TPU v7x, 256 devices: a whole 4x4x8 slice. The times are simulated.
256 devices in a mesh: rep: 2 (over core), expert: 128 (over z, y, x).
Axes of the slice: x: 4, y: 4, z: 8, core: 2. Of those that a mesh axis runs over, the one named last changes fastest.
Arguments:
- tokens: bfloat16 [32768, 1024], P(('rep', 'expert')), may hold values from -6 to 6
- cotangent: bfloat16 [32768, 1024], P(('rep', 'expert')), may hold values from -6 to 6
- gate_values: float32 [32768, 2], P(('rep', 'expert')), may hold values from 0.2 to 1
- expert_ids: int32 [32768, 2], P(('rep', 'expert')), may hold values from 0 to 127, all different within a row; in each aligned block of 128 rows (0 to 127, 128 to 255, ...) at most 4 rows name the same one
- keep_second: int32 [32768], P(('rep', 'expert')), may hold values 0 or 1
- weight_in: bfloat16 [128, 1024, 1024], P('expert'), may hold values from -0.1875 to 0.1875
- weight_out: bfloat16 [128, 1024, 1024], P('expert'), may hold values from -0.1875 to 0.1875
Outputs:
- grad_tokens: bfloat16 [32768, 1024], P(('rep', 'expert'))
- grad_gates: float32 [32768, 2], P(('rep', 'expert'))
- grad_weight_in: bfloat16 [128, 1024, 1024], P('expert', None, 'rep')
- grad_weight_out: bfloat16 [128, 1024, 1024], P('expert', None, 'rep')
Inputs may be any that keep to these rules, and one draw needn't show every extreme that they name: `expert_ids`: in each group of 128 tokens no expert is named by more than 4 tokens, a bound that some block reaches; a token's two experts differ.
All inputs are finite; a program needn't handle non-finite values. No bound on the sum of `keep_second` on one device may be relied on, other than what follows from the above.
Results may differ from a plain program's by a relative error of at most 0.022.
Values may be sent and summed in bfloat16 or wider, within the bound.
A program may use at most 128 MiB of HBM per device.

v0:
```python
import jax
import jax.numpy as jnp
from jax import lax
from jax.sharding import PartitionSpec as P


def gelu_value(pre):
    const = 0.7978845608028654
    inner = jnp.tanh(const * (pre + 0.044715 * pre * pre * pre))
    return 0.5 * pre * (1.0 + inner)


def gelu_slope(pre):
    const = 0.7978845608028654
    inner = jnp.tanh(const * (pre + 0.044715 * pre * pre * pre))
    return 0.5 * (1.0 + inner) + 0.5 * pre * (1.0 - inner * inner) * const * (
        1.0 + 3.0 * 0.044715 * pre * pre
    )


def body(tokens, cotangent, gate_values, expert_ids, keep_second, weight_in, weight_out):
    rows_here = tokens.shape[0]
    width = tokens.shape[1]
    hidden = weight_in.shape[2]
    expert_count = lax.axis_size("expert")
    capacity = max(2, 4 * rows_here // expert_count)
    assign_exp = jnp.concatenate([expert_ids[:, 0], expert_ids[:, 1]])
    onehot = (assign_exp[:, None] == jnp.arange(expert_count, dtype=jnp.int32)[None, :]).astype(
        jnp.int32
    )
    before = jnp.cumsum(onehot, axis=0) - onehot
    position = jnp.sum(before * onehot, axis=1)
    slot = assign_exp * capacity + position
    source_of = (
        jnp.full((expert_count * capacity,), 2 * rows_here, jnp.int32)
        .at[slot]
        .set(jnp.arange(2 * rows_here, dtype=jnp.int32))
    )
    token_of_slot = jnp.where(source_of < 2 * rows_here, source_of % rows_here, rows_here)
    keep_float = keep_second.astype(jnp.float32)
    scale_assign = jnp.concatenate(
        [gate_values[:, 0], gate_values[:, 1] * keep_float, jnp.zeros((1,), jnp.float32)]
    )
    x_padded = jnp.concatenate([tokens, jnp.zeros((1, width), tokens.dtype)], axis=0)
    cot_padded = jnp.concatenate([cotangent, jnp.zeros((1, width), cotangent.dtype)], axis=0)
    x_send = x_padded[token_of_slot].reshape(expert_count, capacity, width)
    cot_send = cot_padded[token_of_slot].reshape(expert_count, capacity, width)
    scale_send = scale_assign[source_of].reshape(expert_count, capacity)
    x_recv, cot_recv, scale_recv = (
        lax.all_to_all(x_send, "expert", split_axis=0, concat_axis=0, tiled=True),
        lax.all_to_all(cot_send, "expert", split_axis=0, concat_axis=0, tiled=True),
        lax.all_to_all(
            scale_send.astype(jnp.bfloat16), "expert", split_axis=0, concat_axis=0, tiled=True
        ).astype(scale_send.dtype),
    )
    proj_in = weight_in[0]
    proj_out = weight_out[0]
    replica_count = lax.axis_size("rep")
    replica_index = lax.axis_index("rep")
    x_rows = x_recv.reshape(-1, width)
    cot_rows = cot_recv.reshape(-1, width)
    scale_rows = scale_recv.reshape(-1)
    pre = jnp.dot(x_rows, proj_in, preferred_element_type=jnp.float32)
    act = gelu_value(pre).astype(jnp.bfloat16)
    outval = jnp.dot(act, proj_out, preferred_element_type=jnp.float32)
    score = jnp.sum(cot_rows.astype(jnp.float32) * outval, axis=1)
    grad_output = (scale_rows[:, None] * cot_rows.astype(jnp.float32)).astype(jnp.bfloat16)
    grad_act = jnp.dot(grad_output, proj_out.T, preferred_element_type=jnp.float32)
    grad_pre = (grad_act * gelu_slope(pre)).astype(jnp.bfloat16)
    grad_assign = jnp.dot(grad_pre, proj_in.T, preferred_element_type=jnp.float32).astype(
        jnp.bfloat16
    )
    grad_in_part = jnp.dot(x_rows.T, grad_pre, preferred_element_type=jnp.float32)
    grad_out_part = jnp.dot(act.T, grad_output, preferred_element_type=jnp.float32)
    sum_in, sum_out = (
        lax.psum(grad_in_part.astype(jnp.bfloat16), "rep").astype(jnp.float32),
        lax.psum(grad_out_part.astype(jnp.bfloat16), "rep").astype(jnp.float32),
    )
    in_share = lax.dynamic_slice_in_dim(
        sum_in, replica_index * (hidden // replica_count), hidden // replica_count, 1
    )
    out_share = lax.dynamic_slice_in_dim(
        sum_out, replica_index * (width // replica_count), width // replica_count, 1
    )
    grad_back, score_back = (
        lax.all_to_all(
            grad_assign.reshape(expert_count, capacity, width),
            "expert",
            split_axis=0,
            concat_axis=0,
            tiled=True,
        ),
        lax.all_to_all(
            score.reshape(expert_count, capacity).astype(jnp.bfloat16),
            "expert",
            split_axis=0,
            concat_axis=0,
            tiled=True,
        ).astype(jnp.float32),
    )
    grad_flat = grad_back.reshape(-1, width)
    score_flat = score_back.reshape(-1)
    first_grad = grad_flat[slot[:rows_here]].astype(jnp.float32)
    second_grad = grad_flat[slot[rows_here:]].astype(jnp.float32)
    grad_tokens = (first_grad + second_grad).astype(jnp.bfloat16)
    grad_gates = jnp.stack(
        [score_flat[slot[:rows_here]], score_flat[slot[rows_here:]] * keep_float], axis=1
    )
    return (
        grad_tokens,
        grad_gates,
        in_share.astype(jnp.bfloat16)[None],
        out_share.astype(jnp.bfloat16)[None],
    )


def solution(mesh):
    in_specs = (
        P(("rep", "expert"), None),
        P(("rep", "expert"), None),
        P(("rep", "expert"), None),
        P(("rep", "expert"), None),
        P(("rep", "expert")),
        P("expert", None, None),
        P("expert", None, None),
    )
    out_specs = (
        P(("rep", "expert"), None),
        P(("rep", "expert"), None),
        P("expert", None, "rep"),
        P("expert", None, "rep"),
    )
    return jax.shard_map(body, mesh=mesh, in_specs=in_specs, out_specs=out_specs, check_vma=False)
```

profile of v0, /device:TPU:2, one launch (start us, length us, event | category | flops | bytes accessed | tf_op | source)
XLA Modules:
  0.0 206.1 jit_solution(7098511506435007507)
XLA Ops:
  8.7 1.4 scatter_custom_fusion
  11.5 3.5 %gather_fusion = bf16[512]{0:T(512)(128)(2,1)S(1)} fusion(bf16[257]{0:T(512)(128)(2,1)S(1)} %pad_maximum_fusion, s32[1024]{0:T(1024)S(1)} %get-tuple-element.17), kind=kCustom, calls=%fused_computation | custom fusion | bytes 4096 | tf_op jit(solution)/shard_map/gather | solution.py:48
  15.8 15.4 %all-to-all-start = ((bf16[128,1,4]{2,1,0:T(2,128)(2,1)}), bf16[128,1,4]{2,1,0:T(2,128)(2,1)S(1)}, u32[]{:S(2)}, u32[]{:S(2)}) async-start(bf16[128,1,4]{2,1,0:T(2,128)(2,1)} %convert_element_type.148), calls=%async_computation | async-start | bytes 131072 | tf_op jit(solution)/shard_map/all_to_all | solution.py:52
  31.3 2.1 gather_fusion.1
  34.6 7.9 %all-to-all-done = bf16[128,1,4]{2,1,0:T(2,128)(2,1)S(1)} async-done(((bf16[128,1,4]{2,1,0:T(2,128)(2,1)}), bf16[128,1,4]{2,1,0:T(2,128)(2,1)S(1)}, u32[]{:S(2)}, u32[]{:S(2)}) %all-to-all-start) | async-done | bytes 1056 | tf_op jit(solution)/shard_map/all_to_all | solution.py:52
  42.5 6.6 %all-to-all-start.1 = ((bf16[128,4,1024]{2,1,0:T(4,128)(2,1)}), bf16[128,4,1024]{2,1,0:T(4,128)(2,1)S(1)}, u32[]{:S(2)}, u32[]{:S(2)}) async-start(bf16[128,4,1024]{2,1,0:T(4,128)(2,1)} %reshape.132), calls=%async_computation.1 | async-start | bytes 2097152 | tf_op jit(solution)/shard_map/all_to_all | solution.py:51
  50.1 2.8 %gather_fusion.2 = bf16[512,1024]{1,0:T(8,128)(2,1)} fusion(bf16[129,1024]{1,0:T(8,128)(2,1)S(1)} %concatenate.25, s32[1024]{0:T(1024)S(1)} %get-tuple-element.16), kind=kCustom, calls=%fused_computation.2 | custom fusion | bytes 2099200 | tf_op jit(solution)/shard_map/gather | solution.py:46
  52.9 2.2 %reshape.133 = bf16[128,4,1024]{2,1,0:T(4,128)(2,1)} reshape(bf16[512,1024]{1,0:T(8,128)(2,1)} %gather_fusion.2) | data formatting | bytes 2097152 | tf_op jit(solution)/shard_map/reshape | solution.py:46
  55.1 23.6 %all-to-all-done.1 = bf16[128,4,1024]{2,1,0:T(4,128)(2,1)S(1)} async-done(((bf16[128,4,1024]{2,1,0:T(4,128)(2,1)}), bf16[128,4,1024]{2,1,0:T(4,128)(2,1)S(1)}, u32[]{:S(2)}, u32[]{:S(2)}) %all-to-all-start.1) | async-done | bytes 1048608 | tf_op jit(solution)/shard_map/all_to_all | solution.py:51
  78.8 7.7 %all-to-all-start.2 = ((bf16[128,4,1024]{2,1,0:T(4,128)(2,1)}), bf16[128,4,1024]{2,1,0:T(4,128)(2,1)}, u32[]{:S(2)}, u32[]{:S(2)}) async-start(bf16[128,4,1024]{2,1,0:T(4,128)(2,1)} %reshape.133), calls=%async_computation.2 | async-start | bytes 2097152 | tf_op jit(solution)/shard_map/all_to_all | solution.py:50
  87.1 1.5 multiply_convert_fusion.2
  88.5 2.2 %convert_element_type.122 = bf16[512,1024]{1,0:T(8,128)(2,1)} reshape(bf16[128,4,1024]{2,1,0:T(4,128)(2,1)} %multiply_convert_fusion.2) | data formatting | bytes 2097152 | tf_op jit(solution)/shard_map/convert_element_type | solution.py:67
  90.7 24.3 %all-to-all-done.2 = bf16[128,4,1024]{2,1,0:T(4,128)(2,1)} async-done(((bf16[128,4,1024]{2,1,0:T(4,128)(2,1)}), bf16[128,4,1024]{2,1,0:T(4,128)(2,1)}, u32[]{:S(2)}, u32[]{:S(2)}) %all-to-all-start.2) | async-done | bytes 1048608 | tf_op jit(solution)/shard_map/all_to_all | solution.py:50
  115.0 2.1 %reshape.134 = bf16[512,1024]{1,0:T(8,128)(2,1)} reshape(bf16[128,4,1024]{2,1,0:T(4,128)(2,1)} %all-to-all-done.2) | data formatting | bytes 2097152 | tf_op jit(solution)/shard_map/reshape | solution.py:60
  117.2 2.6 %fusion.9 = f32[512,1024]{1,0:T(8,128)S(1)} fusion(bf16[512,1024]{1,0:T(8,128)(2,1)} %reshape.134, bf16[1,1024,1024]{2,1,0:T(8,128)(2,1)S(1)} %copy-done), kind=kOutput, calls=%fused_computation.19 | convolution fusion | flops 1073741824 | bytes 5242880 | tf_op jit(solution)/shard_map/dot_general | solution.py:63
  119.8 2.2 %fusion.6 = bf16[512,1024]{1,0:T(8,128)(2,1)S(1)} fusion(f32[512,1024]{1,0:T(8,128)S(1)} %fusion.9, bf16[512,1024]{1,0:T(8,128)(2,1)S(1)} %copy-done.1, bf16[1,1024,1024]{2,1,0:T(8,128)(2,1)S(1)} %copy-done.5), kind=kOutput, calls=%fused_computation.16 | convolution fusion | flops 1083703296 | bytes 6291456 | tf_op jit(solution)/shard_map/dot_general | solution.py:68
  123.1 2.6 %convolution_convert_fusion.1 = bf16[1024,1024]{1,0:T(8,128)(2,1)} fusion(bf16[512,1024]{1,0:T(8,128)(2,1)S(1)} %copy-done.2, bf16[512,1024]{1,0:T(8,128)(2,1)S(1)} %fusion.6), kind=kOutput, calls=%fused_computation.32 | convolution fusion | flops 1074790400 | bytes 4194304 | tf_op jit(solution)/shard_map/dot_general | solution.py:73
  125.7 1.4 reshape.138
  127.1 5.1 %convolution_convert_fusion = bf16[1024,1024]{1,0:T(8,128)(2,1)} fusion(f32[512,1024]{1,0:T(8,128)} %reshape.138, f32[512]{0:T(512)S(1)} %reshape.140, f32[512,1024]{1,0:T(8,128)} %copy-done.7), kind=kOutput, calls=%fused_computation.31 | convolution fusion | flops 1080557568 | bytes 6293504 | tf_op jit(solution)/shard_map/dot_general | solution.py:74
  132.3 4.4 %multiply_reduce_fusion = bf16[512]{0:T(512)(128)(2,1)S(1)} fusion(f32[512,1024]{1,0:T(8,128)} %reshape.138, bf16[1,1024,1024]{2,1,0:T(8,128)(2,1)} %param.13, f32[512,1024]{1,0:T(8,128)} %copy-done.7), kind=kOutput, calls=%fused_computation.28 | convolution fusion | flops 1079508480 | bytes 6292480 | tf_op jit(solution)/shard_map/dot_general | solution.py:65
  137.4 6.6 %all-to-all-start.4 = ((bf16[128,1,4]{2,1,0:T(2,128)(2,1)}), bf16[128,1,4]{2,1,0:T(2,128)(2,1)S(1)}, u32[]{:S(2)}, u32[]{:S(2)}) async-start(bf16[128,1,4]{2,1,0:T(2,128)(2,1)} %convert_element_type.149), calls=%async_computation.4 | async-start | bytes 131072 | tf_op jit(solution)/shard_map/all_to_all | solution.py:93
  144.1 2.5 %fusion.17 = bf16[512,1024]{1,0:T(8,128)(2,1)S(1)} fusion(bf16[512,1024]{1,0:T(8,128)(2,1)} %copy-done.8, bf16[1,1024,1024]{2,1,0:T(8,128)(2,1)S(1)} %copy-done), kind=kOutput, calls=%fused_computation.33 | convolution fusion | flops 1074266112 | bytes 4194304 | tf_op jit(solution)/shard_map/dot_general | solution.py:70
  146.6 1.2 reshape.135
  147.8 7.6 %all-to-all-done.4 = bf16[128,1,4]{2,1,0:T(2,128)(2,1)S(1)} async-done(((bf16[128,1,4]{2,1,0:T(2,128)(2,1)}), bf16[128,1,4]{2,1,0:T(2,128)(2,1)S(1)}, u32[]{:S(2)}, u32[]{:S(2)}) %all-to-all-start.4) | async-done | bytes 1056 | tf_op jit(solution)/shard_map/all_to_all | solution.py:93
  155.4 7.9 %all-to-all-start.3 = ((bf16[128,4,1024]{2,1,0:T(4,128)(2,1)}), bf16[128,4,1024]{2,1,0:T(4,128)(2,1)}, u32[]{:S(2)}, u32[]{:S(2)}) async-start(bf16[128,4,1024]{2,1,0:T(4,128)(2,1)} %reshape.135), calls=%async_computation.3 | async-start | bytes 2097152 | tf_op jit(solution)/shard_map/all_to_all | solution.py:86
  163.7 1.3 gather_fusion.6
  164.9 1.3 gather_fusion.5
  166.8 23.5 %all-to-all-done.3 = bf16[128,4,1024]{2,1,0:T(4,128)(2,1)} async-done(((bf16[128,4,1024]{2,1,0:T(4,128)(2,1)}), bf16[128,4,1024]{2,1,0:T(4,128)(2,1)}, u32[]{:S(2)}, u32[]{:S(2)}) %all-to-all-start.3) | async-done | bytes 1048608 | tf_op jit(solution)/shard_map/all_to_all | solution.py:86
  190.3 1.3 reshape.136
  192.5 1.6 gather_fusion.3
  194.1 1.7 add_convert_fusion
  195.8 2.4 %fusion.22 = bf16[1,1024,512]{2,1,0:T(8,128)(2,1)} fusion(bf16[1024,1024]{1,0:T(8,128)(2,1)} %get-tuple-element.4, s32[]{:T(128)S(6)} %select_n.47), kind=kLoop, calls=%fused_computation.34 | loop fusion | flops 1048576 | bytes 2097156 | tf_op jit(solution)/shard_map/broadcast_in_dim | solution.py:112
  (56 shorter events, 11.0 us)
Async XLA Ops:
  7.2 110.0 %copy-start = (bf16[1,1024,1024]{2,1,0:T(8,128)(2,1)S(1)}, bf16[1,1024,1024]{2,1,0:T(8,128)(2,1)}, u32[]{:S(2)}) copy-start(bf16[1,1024,1024]{2,1,0:T(8,128)(2,1)} %param.12) | copy-start | bytes 6291460
  7.2 24.1 %copy-start.4 = (bf16[128,1024]{1,0:T(8,128)(2,1)S(1)}, bf16[128,1024]{1,0:T(8,128)(2,1)}, u32[]{:S(2)}) copy-start(bf16[128,1024]{1,0:T(8,128)(2,1)} %param.8) | copy-start | bytes 786436
  15.8 26.7 %all-to-all-start = ((bf16[128,1,4]{2,1,0:T(2,128)(2,1)}), bf16[128,1,4]{2,1,0:T(2,128)(2,1)S(1)}, u32[]{:S(2)}, u32[]{:S(2)}) async-start(bf16[128,1,4]{2,1,0:T(2,128)(2,1)} %convert_element_type.148), calls=%async_computation | async-start | bytes 131072 | tf_op jit(solution)/shard_map/all_to_all | solution.py:52
  42.5 36.3 %all-to-all-start.1 = ((bf16[128,4,1024]{2,1,0:T(4,128)(2,1)}), bf16[128,4,1024]{2,1,0:T(4,128)(2,1)S(1)}, u32[]{:S(2)}, u32[]{:S(2)}) async-start(bf16[128,4,1024]{2,1,0:T(4,128)(2,1)} %reshape.132), calls=%async_computation.1 | async-start | bytes 2097152 | tf_op jit(solution)/shard_map/all_to_all | solution.py:51
  78.8 36.3 %all-to-all-start.2 = ((bf16[128,4,1024]{2,1,0:T(4,128)(2,1)}), bf16[128,4,1024]{2,1,0:T(4,128)(2,1)}, u32[]{:S(2)}, u32[]{:S(2)}) async-start(bf16[128,4,1024]{2,1,0:T(4,128)(2,1)} %reshape.133), calls=%async_computation.2 | async-start | bytes 2097152 | tf_op jit(solution)/shard_map/all_to_all | solution.py:50
  86.5 109.3 %all-reduce.5.cloned.1.call-start = ((), (), s32[]{:S(2)}) async-start(), calls=%async_computation.5 | async-start | bytes 8388608 | tf_op jit(solution)/shard_map/psum | solution.py:76
  117.2 2.6 %copy-start.1 = (bf16[512,1024]{1,0:T(8,128)(2,1)S(1)}, bf16[512,1024]{1,0:T(8,128)(2,1)}, u32[]{:S(2)}) copy-start(bf16[512,1024]{1,0:T(8,128)(2,1)} %convert_element_type.122) | copy-start | bytes 3145732
  117.2 2.6 %copy-start.5 = (bf16[1,1024,1024]{2,1,0:T(8,128)(2,1)S(1)}, bf16[1,1024,1024]{2,1,0:T(8,128)(2,1)}, u32[]{:S(2)}) copy-start(bf16[1,1024,1024]{2,1,0:T(8,128)(2,1)} %param.13) | copy-start | bytes 6291460
  119.8 2.3 %copy-start.7 = (f32[512,1024]{1,0:T(8,128)}, f32[512,1024]{1,0:T(8,128)S(1)}, u32[]{:S(2)}) copy-start(f32[512,1024]{1,0:T(8,128)S(1)} %fusion.9) | copy-start | bytes 6291460
  119.8 3.2 %copy-start.2 = (bf16[512,1024]{1,0:T(8,128)(2,1)S(1)}, bf16[512,1024]{1,0:T(8,128)(2,1)}, u32[]{:S(2)}) copy-start(bf16[512,1024]{1,0:T(8,128)(2,1)} %reshape.134) | copy-start | bytes 3145732
  122.1 1.0 copy-start.8
  137.4 18.0 %all-to-all-start.4 = ((bf16[128,1,4]{2,1,0:T(2,128)(2,1)}), bf16[128,1,4]{2,1,0:T(2,128)(2,1)S(1)}, u32[]{:S(2)}, u32[]{:S(2)}) async-start(bf16[128,1,4]{2,1,0:T(2,128)(2,1)} %convert_element_type.149), calls=%async_computation.4 | async-start | bytes 131072 | tf_op jit(solution)/shard_map/all_to_all | solution.py:93
  147.8 18.4 %copy-start.6 = (s32[128]{0:T(128)S(1)}, s32[128]{0:T(128)}, u32[]{:S(2)}) copy-start(s32[128]{0:T(128)} %param.11) | copy-start | bytes 1540
  155.4 34.9 %all-to-all-start.3 = ((bf16[128,4,1024]{2,1,0:T(4,128)(2,1)}), bf16[128,4,1024]{2,1,0:T(4,128)(2,1)}, u32[]{:S(2)}, u32[]{:S(2)}) async-start(bf16[128,4,1024]{2,1,0:T(4,128)(2,1)} %reshape.135), calls=%async_computation.3 | async-start | bytes 2097152 | tf_op jit(solution)/shard_map/all_to_all | solution.py:86
  195.8 2.4 %copy-start.3 = (bf16[1024,1024]{1,0:T(8,128)(2,1)S(1)}, bf16[1024,1024]{1,0:T(8,128)(2,1)}, u32[]{:S(2)}) copy-start(bf16[1024,1024]{1,0:T(8,128)(2,1)} %get-tuple-element.5) | copy-start | bytes 6291460
Sparse Core Ops, SparseCore 0:
  132.4 33.4 all-reduce.4
where the time goes:
time: 207 us; the launch traced here: 206 us
  waiting for transfers between devices  87 us (42%)
  starting transfers between devices  44.5 us (21%)
  local copies, waits for them, and re-layouts  31.9 us (15%)
  matrix products  19.5 us (9%)
  between operations  14.4 us (7%)
  other arithmetic  8.88 us (4%)
    all_to_all x1, waiting for transfers between devices, body(): lax.all_to_all(x_send, 'expert', split_axis=0, concat_axis=0, tiled=True)  24.3 us
    all_to_all x1, waiting for transfers between devices, body(): lax.all_to_all(cot_send, 'expert', split_axis=0, concat_axis=0, tiled=True)  23.6 us
    all_to_all x1, waiting for transfers between devices, body(): lax.all_to_all(grad_assign.reshape(expert_count, capacity, width), 'exper...  23.5 us
    all_to_all x1, starting transfers between devices, body(): lax.all_to_all(scale_send.astype(jnp.bfloat16), 'expert', split_axis=0, c...  15.4 us
    all_to_all x1, waiting for transfers between devices, body(): lax.all_to_all(scale_send.astype(jnp.bfloat16), 'expert', split_axis=0, c...  7.93 us
    all_to_all x1, starting transfers between devices, body(): lax.all_to_all(grad_assign.reshape(expert_count, capacity, width), 'exper...  7.92 us
    all_to_all x1, starting transfers between devices, body(): lax.all_to_all(x_send, 'expert', split_axis=0, concat_axis=0, tiled=True)  7.7 us
    all_to_all x1, waiting for transfers between devices, body(): lax.all_to_all(score.reshape(expert_count, capacity).astype(jnp.bfloat16)...  7.6 us
  transfers between devices with their start and end apart: 6, of which 5 were waited for; matrix products, arithmetic and copies ran while one was open for 15% of the time, Pallas kernels for 0%

commit v1 on v0

v1 whole, which is shorter than its diff:
```python
import functools

import jax
import jax.numpy as jnp
from jax import lax
from jax.experimental import pallas as pl
from jax.experimental.pallas import tpu as pltpu
from jax.sharding import PartitionSpec as P

MESH = pl.DeviceIdType.MESH
F32, BF16, I32 = jnp.float32, jnp.bfloat16, jnp.int32
NZ, NY, NX = 8, 4, 4
PLANE = NY * NX
EXPERTS = NZ * PLANE
CAP = 4
TOK = 128
D = 1024
F = 1024
HALF = 512
ORDER = (3, 5, 4, 0, 2, 6, 1, 7)
CHUNKS = 4
BLOCKS = EXPERTS // CHUNKS
ROWS = BLOCKS * 16
SLOTS = BLOCKS * CAP
SELF_CHUNK, SELF_BLOCK = ORDER.index(0) // 2, (ORDER.index(0) % 2) * PLANE


def dot(a, b, contract):
    return lax.dot_general(a, b, (contract, ((), ())), preferred_element_type=F32)


def iota(shape, dim):
    return lax.broadcasted_iota(I32, shape, dim)


def gelu_parts(pre):
    const = 0.7978845608028654
    square = pre * pre
    inner = jnp.tanh(const * (pre + 0.044715 * square * pre))
    half = 0.5 * (1.0 + inner)
    slope = half + 0.5 * pre * (1.0 - inner * inner) * (
        const * (1.0 + 3.0 * 0.044715 * square)
    )
    return pre * half, slope


def kernel(
    tokens_ref, cot_ref, gates_ref, ids_ref, keep_ref, win_hbm, wout_hbm,
    gtok_ref, ggate_ref, gwin_ref, gwout_ref,
    win, wout, xcat, send, recv, ret, back, score_ret, score_back,
    xrows, gorows, actrows, gprows, perm, wg_send, wg_recv, colcode, total,
    load_sem, self_sem, send_sem, recv_sem, ret_sem, back_sem,
    sret_sem, sback_sem, wgs_sem, wgr_sem,
):
    me = lax.axis_index("expert")
    rep = lax.axis_index("rep")
    my_z, my_y, my_x = me // PLANE, (me // NX) % NY, me % NX

    bar = pltpu.get_barrier_semaphore()

    def greet(i, carry):
        pl.semaphore_signal(bar, inc=1, device_id=(rep, (me + i) % EXPERTS), device_id_type=MESH)
        return carry

    lax.fori_loop(1, EXPERTS, greet, 0)
    pl.semaphore_signal(bar, inc=1, device_id=(1 - rep, me), device_id_type=MESH)

    load_in = pltpu.make_async_copy(win_hbm.at[0], win, load_sem.at[0])
    load_out = pltpu.make_async_copy(wout_hbm.at[0], wout, load_sem.at[1])
    load_in.start()
    load_out.start()

    ids = ids_ref[...]
    dz = (ids // PLANE - my_z + NZ) % NZ
    dy = ((ids // NX) % NY - my_y + NY) % NY
    dx = (ids % NX - my_x + NX) % NX
    pz = jnp.zeros_like(dz)
    for at, off in enumerate(ORDER):
        pz = jnp.where(dz == off, at, pz)
    place = pz * PLANE + dy * NX + dx
    first, second = place[0:1], place[1:2]
    hot0 = jnp.where(iota((EXPERTS, TOK), 0) == first, 1.0, 0.0)
    hot1 = jnp.where(iota((EXPERTS, TOK), 0) == second, 1.0, 0.0)
    upper = jnp.where(iota((TOK, TOK), 0) < iota((TOK, TOK), 1), 1.0, 0.0).astype(BF16)
    plain = ((1,), (0,))
    before0 = dot(hot0.astype(BF16), upper, plain)
    before1 = dot(hot1.astype(BF16), upper, plain) + jnp.sum(hot0, axis=1, keepdims=True)
    pos0 = jnp.sum(hot0 * before0, axis=0, keepdims=True)
    pos1 = jnp.sum(hot1 * before1, axis=0, keepdims=True)
    code0 = first * 16 + pos0.astype(I32)
    code1 = second * 16 + pos1.astype(I32)
    gate_low = gates_ref[...].astype(BF16).astype(F32)
    scale0 = gate_low[0:1]
    scale1 = gate_low[1:2] * keep_ref[...].astype(F32)
    one = jnp.ones_like(scale0)
    quad0 = jnp.concatenate([code0 + 4 * q for q in range(4)], axis=1)
    quad1 = jnp.concatenate([code1 + 4 * q for q in range(4)], axis=1)
    weight0 = jnp.concatenate([one, one, scale0, scale0], axis=1)
    weight1 = jnp.concatenate([one, one, scale1, scale1], axis=1)

    xcat[0:128, :] = tokens_ref[:, 0:HALF]
    xcat[128:256, :] = tokens_ref[:, HALF:]
    xcat[256:384, :] = cot_ref[:, 0:HALF]
    xcat[384:512, :] = cot_ref[:, HALF:]

    def target(c, b, sign):
        lead = b // PLANE
        off = ORDER[2 * c] + (ORDER[2 * c + 1] - ORDER[2 * c]) * lead
        return (
            rep,
            ((my_z + sign * off + NZ) % NZ) * PLANE
            + ((my_y + sign * ((b // NX) % NY) + NY) % NY) * NX
            + (my_x + sign * (b % NX) + NX) % NX,
        )

    def gather(c):
        row = iota((ROWS, 512), 0) + c * ROWS
        pick = jnp.where(row == quad0, weight0, jnp.where(row == quad1, weight1, 0.0))
        block = dot(pick.astype(BF16), xcat[...], plain).astype(BF16)
        send[c] = block.reshape(BLOCKS, 16, HALF)

    def spans(c):
        if c == SELF_CHUNK:
            return [(lo, hi) for lo, hi in ((0, SELF_BLOCK), (SELF_BLOCK + 1, BLOCKS)) if hi > lo]
        return [(0, BLOCKS)]

    def dispatch(c):
        def go(b, carry):
            pltpu.make_async_remote_copy(
                send.at[c, b], recv.at[c, b], send_sem.at[c], recv_sem.at[c],
                device_id=target(c, b, 1), device_id_type=MESH,
            ).start()
            return carry

        for lo, hi in spans(c):
            lax.fori_loop(lo, hi, go, 0)
        if c == SELF_CHUNK:
            pltpu.make_async_copy(
                send.at[c, SELF_BLOCK], recv.at[c, SELF_BLOCK], self_sem.at[0]
            ).start()

    def await_all(buffer, c, sem):
        count = BLOCKS - (c == SELF_CHUNK)
        part = buffer.at[c, pl.ds(0, count)]
        pltpu.make_async_copy(part, part, sem.at[c]).wait()

    gather(0)
    pl.semaphore_wait(bar, EXPERTS)
    dispatch(0)
    for c in range(1, CHUNKS):
        gather(c)
        dispatch(c)

    codes = jnp.concatenate([code0, code1, jnp.zeros((TOK - 2, TOK), I32)], axis=0)
    colcode[...] = jnp.transpose(codes.astype(F32))
    out_row = iota((256, 256), 0)
    in_row = ((out_row // 4) % 16) * 16 + (out_row // 64) * 4 + out_row % 4
    perm[0] = jnp.where(in_row == iota((256, 256), 1), 1.0, 0.0).astype(BF16)
    out_col = iota((256, 256), 1)
    in_col = ((out_col // 4) % 16) * 16 + (out_col // 64) * 4 + out_col % 4
    perm[1] = jnp.where(in_col == iota((256, 256), 0), 1.0, 0.0).astype(BF16)
    load_in.wait()
    load_out.wait()

    for c in range(CHUNKS):
        await_all(recv, c, recv_sem)
        if c == SELF_CHUNK:
            pltpu.make_async_copy(
                send.at[c, SELF_BLOCK], recv.at[c, SELF_BLOCK], self_sem.at[0]
            ).wait()
        base = c * SLOTS
        for g in range(2):
            packed = recv[c, g * 16:(g + 1) * 16].reshape(256, HALF)
            sorted_rows = dot(perm[0], packed, plain).astype(BF16)
            at = slice(base + g * 64, base + (g + 1) * 64)
            xrows[at, 0:HALF] = sorted_rows[0:64]
            xrows[at, HALF:] = sorted_rows[64:128]
            gorows[at, 0:HALF] = sorted_rows[128:192]
            gorows[at, HALF:] = sorted_rows[192:256]
        rows = slice(base, base + SLOTS)
        pre = dot(xrows[rows], win[...], plain)
        grad_act = dot(gorows[rows], wout[...], ((1,), (1,)))
        act, slope = gelu_parts(pre)
        act = act.astype(BF16)
        actrows[rows] = act
        grad_pre = (grad_act * slope).astype(BF16)
        gprows[rows] = grad_pre
        score = jnp.sum(act.astype(F32) * grad_act, axis=1, keepdims=True)
        spread = jnp.where(iota((SLOTS, 128), 0) % CAP == iota((SLOTS, 128), 1), score, 0.0)
        high = spread.astype(BF16)
        low = (spread - high.astype(F32)).astype(BF16)
        group = jnp.where(
            iota((BLOCKS, SLOTS), 1) // CAP == iota((BLOCKS, SLOTS), 0), 1.0, 0.0
        ).astype(BF16)
        score_ret[c] = (dot(group, high, plain) + dot(group, low, plain)).reshape(BLOCKS, 1, 128)
        grad_rows = dot(grad_pre, win[...], ((1,), (1,))).astype(BF16)
        for g in range(2):
            part = grad_rows[g * 64:(g + 1) * 64]
            stack = jnp.concatenate([part[:, q * 256:(q + 1) * 256] for q in range(4)], axis=0)
            mixed = dot(perm[1], stack, plain).astype(BF16)
            ret[c, g * 16:(g + 1) * 16] = mixed.reshape(16, 16, 256)

        def give(b, carry, c=c):
            to = target(c, b, -1)
            pltpu.make_async_remote_copy(
                ret.at[c, b], back.at[c, b], ret_sem.at[c], back_sem.at[c],
                device_id=to, device_id_type=MESH,
            ).start()
            pltpu.make_async_remote_copy(
                score_ret.at[c, b], score_back.at[c, b], sret_sem.at[c], sback_sem.at[c],
                device_id=to, device_id_type=MESH,
            ).start()
            return carry

        for lo, hi in spans(c):
            lax.fori_loop(lo, hi, give, 0)
        if c == SELF_CHUNK:
            pltpu.make_async_copy(
                ret.at[c, SELF_BLOCK], back.at[c, SELF_BLOCK], self_sem.at[1]
            ).start()
            pltpu.make_async_copy(
                score_ret.at[c, SELF_BLOCK], score_back.at[c, SELF_BLOCK], self_sem.at[2]
            ).start()

    theirs = pl.multiple_of((1 - rep) * HALF, HALF)
    mine = pl.multiple_of(rep * HALF, HALF)
    down = ((0,), (0,))
    wg_send[0] = dot(xrows[...], gprows[:, pl.ds(theirs, HALF)], down).astype(BF16)
    wg_send[1] = dot(actrows[...], gorows[:, pl.ds(theirs, HALF)], down).astype(BF16)
    swap = pltpu.make_async_remote_copy(
        wg_send, wg_recv, wgs_sem, wgr_sem, device_id=(1 - rep, me), device_id_type=MESH
    )
    swap.start()
    own_in = dot(xrows[...], gprows[:, pl.ds(mine, HALF)], down)
    own_out = dot(actrows[...], gorows[:, pl.ds(mine, HALF)], down)
    swap.wait()
    gwin_ref[0] = (own_in + wg_recv[0].astype(F32)).astype(BF16)
    gwout_ref[0] = (own_out + wg_recv[1].astype(F32)).astype(BF16)

    col0 = colcode[:, 0:1].astype(I32)
    col1 = colcode[:, 1:2].astype(I32)
    for c in range(CHUNKS):
        await_all(back, c, back_sem)
        if c == SELF_CHUNK:
            pltpu.make_async_copy(
                ret.at[c, SELF_BLOCK], back.at[c, SELF_BLOCK], self_sem.at[1]
            ).wait()
        lane = iota((TOK, ROWS), 1) + c * ROWS
        landed = back[c].reshape(ROWS, 256)
        for q in range(4):
            pick = jnp.where(lane == col0 + 4 * q, 1.0, jnp.where(lane == col1 + 4 * q, 1.0, 0.0))
            part = dot(pick.astype(BF16), landed, plain)
            if c == 0:
                total[:, q * 256:(q + 1) * 256] = part
            else:
                total[:, q * 256:(q + 1) * 256] += part
    gtok_ref[...] = total[...].astype(BF16)
    for c in range(CHUNKS):
        await_all(score_back, c, sback_sem)
    pltpu.make_async_copy(
        score_ret.at[SELF_CHUNK, SELF_BLOCK], score_back.at[SELF_CHUNK, SELF_BLOCK], self_sem.at[2]
    ).wait()
    scores = score_back[...].reshape(EXPERTS, 128)
    got0 = jnp.zeros((1, TOK), F32)
    got1 = jnp.zeros((1, TOK), F32)
    for s in range(CAP):
        column = scores[:, s:s + 1]
        got0 = got0 + jnp.where(pos0 == s, jnp.sum(hot0 * column, axis=0, keepdims=True), 0.0)
        got1 = got1 + jnp.where(pos1 == s, jnp.sum(hot1 * column, axis=0, keepdims=True), 0.0)
    ggate_ref[...] = jnp.concatenate([got0, got1], axis=0) / gate_low

    for c in range(CHUNKS):
        await_all(send, c, send_sem)
        await_all(ret, c, ret_sem)
        await_all(score_ret, c, sret_sem)


def body(tokens, cotangent, gate_values, expert_ids, keep_second, weight_in, weight_out):
    vmem = pl.BlockSpec(memory_space=pltpu.VMEM)
    hbm = pl.BlockSpec(memory_space=pl.ANY)
    dma = pltpu.SemaphoreType.DMA
    flops = 2 * 512 * 1024 * 1024 * 6
    grad_tokens, grad_gates, grad_in, grad_out = pl.pallas_call(
        kernel,
        out_shape=(
            jax.ShapeDtypeStruct((TOK, D), BF16),
            jax.ShapeDtypeStruct((2, TOK), F32),
            jax.ShapeDtypeStruct((1, D, HALF), BF16),
            jax.ShapeDtypeStruct((1, F, HALF), BF16),
        ),
        in_specs=[vmem] * 5 + [hbm] * 2,
        out_specs=(vmem,) * 4,
        scratch_shapes=[
            pltpu.VMEM((D, F), BF16),
            pltpu.VMEM((F, D), BF16),
            pltpu.VMEM((512, HALF), BF16),
            pltpu.VMEM((CHUNKS, BLOCKS, 16, HALF), BF16),
            pltpu.VMEM((CHUNKS, BLOCKS, 16, HALF), BF16),
            pltpu.VMEM((CHUNKS, BLOCKS, 16, 256), BF16),
            pltpu.VMEM((CHUNKS, BLOCKS, 16, 256), BF16),
            pltpu.VMEM((CHUNKS, BLOCKS, 1, 128), F32),
            pltpu.VMEM((CHUNKS, BLOCKS, 1, 128), F32),
            pltpu.VMEM((512, D), BF16),
            pltpu.VMEM((512, D), BF16),
            pltpu.VMEM((512, F), BF16),
            pltpu.VMEM((512, F), BF16),
            pltpu.VMEM((2, 256, 256), BF16),
            pltpu.VMEM((2, D, HALF), BF16),
            pltpu.VMEM((2, D, HALF), BF16),
            pltpu.VMEM((TOK, TOK), F32),
            pltpu.VMEM((TOK, D), F32),
            dma((2,)), dma((3,)),
            dma((CHUNKS,)), dma((CHUNKS,)), dma((CHUNKS,)), dma((CHUNKS,)),
            dma((CHUNKS,)), dma((CHUNKS,)), dma, dma,
        ],
        compiler_params=pltpu.CompilerParams(
            collective_id=0, has_side_effects=True, vmem_limit_bytes=56 * 2**20
        ),
        cost_estimate=pl.CostEstimate(
            flops=flops, bytes_accessed=7 * 2**20, transcendentals=512 * 1024
        ),
    )(
        tokens,
        cotangent,
        gate_values.T,
        expert_ids.T,
        keep_second.reshape(1, TOK),
        weight_in,
        weight_out,
    )
    return grad_tokens, grad_gates.T, grad_in, grad_out


def solution(mesh):
    in_specs = (
        P(("rep", "expert"), None),
        P(("rep", "expert"), None),
        P(("rep", "expert"), None),
        P(("rep", "expert"), None),
        P(("rep", "expert")),
        P("expert", None, None),
        P("expert", None, None),
    )
    out_specs = (
        P(("rep", "expert"), None),
        P(("rep", "expert"), None),
        P("expert", None, "rep"),
        P("expert", None, "rep"),
    )
    return jax.shard_map(body, mesh=mesh, in_specs=in_specs, out_specs=out_specs, check_vma=False)
```

time: 207 us -> 96.4 us (0.47)
  Pallas kernels: 0 us -> 88.1 us
  waiting for transfers between devices: 87 us -> 0 us
  starting transfers between devices: 44.5 us -> 0 us
  local copies, waits for them, and re-layouts: 31.9 us -> 6.23 us
  matrix products: 19.5 us -> 0 us
  between operations: 14.4 us -> 0.65 us
  other arithmetic: 8.88 us -> 0 us
    pallas_call x0 -> x1, Pallas kernels: none -> 88.1 us  [body(): pl.pallas_call(kernel, out_shape=(jax.ShapeDtypeStruct((TOK, D), BF16), j...]
    all_to_all x5 -> x0, waiting for transfers between devices: 87 us -> none  [the longest x1 24.3 us: body(): lax.all_to_all(x_send, 'expert', split_axis=0, concat_axis=0, tiled=True)]
    all_to_all x5 -> x0, starting transfers between devices: 44.3 us -> none  [the longest x1 15.4 us: body(): lax.all_to_all(scale_send.astype(jnp.bfloat16), 'expert', split_axis=0, c...]
    dot_general x6 -> x0, matrix products: 19.5 us -> none  [the longest x1 5.14 us: body(): jnp.dot(act.T, grad_output, preferred_element_type=jnp.float32)]
    gather x7 -> x0, local copies, waits for them, and re-layouts: 13.3 us -> none  [the longest x1 3.51 us: body(): scale_send = scale_assign[source_of].reshape(expert_count, capacity)]
    reshape x5 -> x0, local copies, waits for them, and re-layouts: 8.13 us -> none  [the longest x1 2.24 us: body(): x_send = x_padded[token_of_slot].reshape(expert_count, capacity, width)]
    convert_element_type x6 -> x0, local copies, waits for them, and re-layouts: 5.34 us -> none  [the longest x1 2.2 us: body(): (scale_rows[:, None] * cot_rows.astype(jnp.float32)).astype(jnp.bfloat16)]
    unnamed x19 -> x6, local copies, waits for them, and re-layouts: 1.01 us -> 6.23 us
  transfers between devices with their start and end apart: 6 -> 0, of which waited for: 5 -> 0; matrix products, arithmetic and copies ran while one was open for 15% -> 0% of each run, Pallas kernels for 0% -> 0%
where the time goes in v1:
time: 96.4 us; the launch traced here: 95 us
  Pallas kernels  88.1 us (91%)
  local copies, waits for them, and re-layouts  6.23 us (6%)
    pallas_call x1, Pallas kernels, body(): pl.pallas_call(kernel, out_shape=(jax.ShapeDtypeStruct((TOK, D), BF16), j...  88.1 us
    unnamed x6, local copies, waits for them, and re-layouts  6.23 us

profile of v1, /device:TPU:2, one launch (start us, length us, event | category | flops | bytes accessed | tf_op | source)
XLA Modules:
  0.0 95.0 jit_solution(15182772420185442374)
XLA Ops:
  0.6 88.1 %shard_map.102 = (bf16[128,1024]{1,0:T(8,128)(2,1)}, f32[2,128]{1,0:T(2,128)}, bf16[1,1024,512]{2,1,0:T(8,128)(2,1)}, bf16[1,1024,512]{2,1,0:T(8,128)(2,1)}) custom-call(bf16[128,1024]{1,0:T(8,128)(2,1)} %tokens_ref.1, bf16[128,1024]{1,0:T(8,128)(2,1)} %cot_ref.1, f32[2,128]{1,0:T(2,128)} %bitcast.5, s32[2,128]{1,0:T(2,128)} %bitcast.6, s32[1,128]{1,0:T(1,128)} %bitcast.7, ...), custom_call_target="tpu_custom_call" | custom-call | flops 6442450944 | bytes 7340032 | tf_op jit(solution)/shard_map/pallas_call | solution.py:283
  88.8 0.0 copy-start
  88.8 1.8 %copy.15 = bf16[128,1024]{1,0:T(8,128)(2,1)} copy(bf16[128,1024]{1,0:T(8,128)(2,1)} %get-tuple-element.16) | data formatting | bytes 524288
  90.5 1.2 %copy.16 = f32[128,2]{0,1:T(2,128)} copy(f32[128,2]{0,1:T(2,128)} %bitcast.4) | data formatting | bytes 2048
  91.8 2.3 %copy.17 = bf16[1,1024,512]{2,1,0:T(8,128)(2,1)} copy(bf16[1,1024,512]{2,1,0:T(8,128)(2,1)} %get-tuple-element.18) | data formatting | bytes 2097152
  94.0 0.0 copy-done
  94.0 1.0 %copy.18 = bf16[1,1024,512]{2,1,0:T(8,128)(2,1)} copy(bf16[1,1024,512]{2,1,0:T(8,128)(2,1)S(1)} %copy-done) | data formatting | bytes 2097152
Async XLA Ops:
  88.8 5.3 %copy-start = (bf16[1,1024,512]{2,1,0:T(8,128)(2,1)S(1)}, bf16[1,1024,512]{2,1,0:T(8,128)(2,1)}, u32[]{:S(2)}) copy-start(bf16[1,1024,512]{2,1,0:T(8,128)(2,1)} %get-tuple-element.19) | copy-start | bytes 3145732

commit v2 on v1

v2 whole, which is shorter than its diff:
```python
import functools

import jax
import jax.numpy as jnp
from jax import lax
from jax.experimental import pallas as pl
from jax.experimental.pallas import tpu as pltpu
from jax.sharding import PartitionSpec as P

MESH = pl.DeviceIdType.MESH
F32, BF16, I32 = jnp.float32, jnp.bfloat16, jnp.int32
NZ, NY, NX = 8, 4, 4
PLANE = NY * NX
EXPERTS = NZ * PLANE
CAP = 4
TOK = 128
D = 1024
F = 1024
HALF = 512
ORDER = (0, 4, 3, 5, 2, 6, 1, 7)
CHUNKS = 4
BLOCKS = EXPERTS // CHUNKS
ROWS = BLOCKS * 16
SLOTS = BLOCKS * CAP
RUNS = (
    ((0, 16, 0, 0), (16, 24, 1, 3), (24, 32, 2, -3)),
    ((0, 16, 1, 2), (16, 32, 2, -2)),
    ((0, 16, 1, 1), (16, 32, 2, -1)),
    ((0, 16, 1, 0), (16, 32, 2, 0)),
)
STAY = ((0, 0), (3, 0), (3, 16))


def dot(a, b, contract):
    return lax.dot_general(a, b, (contract, ((), ())), preferred_element_type=F32)


def iota(shape, dim):
    return lax.broadcasted_iota(I32, shape, dim)


def gelu_parts(pre):
    const = 0.7978845608028654
    square = pre * pre
    inner = jnp.tanh(const * (pre + 0.044715 * square * pre))
    half = 0.5 * (1.0 + inner)
    slope = half + 0.5 * pre * (1.0 - inner * inner) * (
        const * (1.0 + 3.0 * 0.044715 * square)
    )
    return pre * half, slope


def kernel(
    tokens_hbm, cot_hbm, gates_hbm, ids_hbm, keep_hbm, win_hbm, wout_hbm,
    gtok_ref, ggate_ref, gwin_ref, gwout_ref,
    win, wout, win_t, wout_t, gates, ids_in, keep, xcat, xnear, meta, meta_near, send, recv, ret, back,
    score_ret, score_back, xrows, gorows, actrows, gprows, perm, wg_send, wg_recv,
    colcode, total, part_send, part_recv, score_send, score_recv,
    load_sem, near_send, near_recv, stay_sem, send_sem, recv_sem, ret_sem, back_sem,
    sret_sem, sback_sem, part_ssem, part_rsem, wgs_sem, wgr_sem,
):
    me = lax.axis_index("expert")
    rep = lax.axis_index("rep")
    my_z, my_y, my_x = me // PLANE, (me // NX) % NY, me % NX

    def device(dz, dy, dx):
        return (
            rep,
            ((my_z + dz + NZ) % NZ) * PLANE
            + ((my_y + dy + NY) % NY) * NX
            + (my_x + dx + NX) % NX,
        )

    def near(side):
        return device(1 - 2 * side, 0, 0)

    loads = [
        pltpu.make_async_copy(ids_hbm, ids_in, load_sem.at[0]),
        pltpu.make_async_copy(gates_hbm, gates, load_sem.at[1]),
        pltpu.make_async_copy(keep_hbm, keep, load_sem.at[2]),
        pltpu.make_async_copy(tokens_hbm.at[:, 0:HALF], xcat.at[0:128], load_sem.at[3]),
        pltpu.make_async_copy(tokens_hbm.at[:, HALF:D], xcat.at[128:256], load_sem.at[4]),
        pltpu.make_async_copy(cot_hbm.at[:, 0:HALF], xcat.at[256:384], load_sem.at[5]),
        pltpu.make_async_copy(cot_hbm.at[:, HALF:D], xcat.at[384:512], load_sem.at[6]),
        pltpu.make_async_copy(win_hbm.at[0], win, load_sem.at[7]),
        pltpu.make_async_copy(wout_hbm.at[0], wout, load_sem.at[8]),
    ]
    for load in loads[:7]:
        load.start()

    bar = pltpu.get_barrier_semaphore()

    def greet(i, carry):
        to = device(i // PLANE - 3, (i // NX) % NY, i % NX)
        pl.semaphore_signal(bar, inc=1, device_id=to, device_id_type=MESH)
        return carry

    lax.fori_loop(0, 3 * PLANE, greet, 0)
    lax.fori_loop(3 * PLANE + 1, 7 * PLANE, greet, 0)
    pl.semaphore_signal(bar, inc=1, device_id=(1 - rep, me), device_id_type=MESH)
    for load in loads[7:]:
        load.start()

    for load in loads[:3]:
        load.wait()
    ids = ids_in[...]
    dz = (ids // PLANE - my_z + NZ) % NZ
    dy = ((ids // NX) % NY - my_y + NY) % NY
    dx = (ids % NX - my_x + NX) % NX
    pz = jnp.zeros_like(dz)
    for at, off in enumerate(ORDER):
        pz = jnp.where(dz == off, at, pz)
    place = pz * PLANE + dy * NX + dx
    first, second = place[0:1], place[1:2]
    hot0 = jnp.where(iota((EXPERTS, TOK), 0) == first, 1.0, 0.0)
    hot1 = jnp.where(iota((EXPERTS, TOK), 0) == second, 1.0, 0.0)
    upper = jnp.where(iota((TOK, TOK), 0) < iota((TOK, TOK), 1), 1.0, 0.0).astype(BF16)
    plain = ((1,), (0,))
    before0 = dot(hot0.astype(BF16), upper, plain)
    before1 = dot(hot1.astype(BF16), upper, plain) + jnp.sum(hot0, axis=1, keepdims=True)
    pos0 = jnp.sum(hot0 * before0, axis=0, keepdims=True)
    pos1 = jnp.sum(hot1 * before1, axis=0, keepdims=True)
    gate_low = gates[...].astype(BF16).astype(F32)
    meta[...] = jnp.concatenate(
        [
            first.astype(F32) * 16 + pos0,
            second.astype(F32) * 16 + pos1,
            gate_low[0:1],
            gate_low[1:2] * keep[...].astype(F32),
            jnp.zeros((4, TOK), F32),
        ],
        axis=0,
    )

    def hand_over(side):
        to = near(side)
        return [
            pltpu.make_async_remote_copy(
                meta, meta_near.at[side], near_send.at[side, 0], near_recv.at[side, 0],
                device_id=to, device_id_type=MESH,
            )
        ] + [
            pltpu.make_async_remote_copy(
                xcat.at[part * 256:(part + 1) * 256],
                xnear.at[side, part * 256:(part + 1) * 256],
                near_send.at[side, 1 + part], near_recv.at[side, 1 + part],
                device_id=to, device_id_type=MESH,
            )
            for part in range(2)
        ]

    handed = [hand_over(0), hand_over(1)]
    for load in loads[3:7]:
        load.wait()
    pl.semaphore_wait(bar, 7 * PLANE)
    for part in range(3):
        for side in range(2):
            handed[side][part].start()

    def quads(source):
        rows = meta[...] if source == 0 else meta_near[source - 1]
        code0, code1 = rows[0:1].astype(I32), rows[1:2].astype(I32)
        one = jnp.ones((1, TOK), F32)
        return (
            jnp.concatenate([code0 + 4 * q for q in range(4)], axis=1),
            jnp.concatenate([code1 + 4 * q for q in range(4)], axis=1),
            jnp.concatenate([one, one, rows[2:3], rows[2:3]], axis=1),
            jnp.concatenate([one, one, rows[3:4], rows[3:4]], axis=1),
        )

    def gather(c, run, quad):
        lo, hi, source, _ = run
        row = iota(((hi - lo) * 16, 512), 0) + (c * BLOCKS + lo) * 16
        pick = jnp.where(row == quad[0], quad[2], jnp.where(row == quad[1], quad[3], 0.0))
        held = xcat[...] if source == 0 else xnear[source - 1]
        block = dot(pick.astype(BF16), held, plain).astype(BF16)
        send[c, lo:hi] = block.reshape(hi - lo, 16, HALF)

    def target(b, off, sign):
        return device(sign * off, sign * ((b // NX) % NY), sign * (b % NX))

    def each(c, run, step):
        lo, hi = run[:2]
        lax.fori_loop(lo + ((c, lo) in STAY), hi, step, 0)

    def dispatch(c, run):
        def go(b, carry):
            pltpu.make_async_remote_copy(
                send.at[c, b], recv.at[c, b], send_sem.at[c], recv_sem.at[c],
                device_id=target(b, run[3], 1), device_id_type=MESH,
            ).start()
            return carry

        each(c, run, go)

    def stay(sources, results, kind, c):
        return [
            pltpu.make_async_copy(sources.at[c, b], results.at[c, b], stay_sem.at[kind, i])
            for i, (at, b) in enumerate(STAY)
            if at == c
        ]

    def await_all(buffer, c, sem):
        count = BLOCKS - sum(at == c for at, _ in STAY)
        part = buffer.at[c, pl.ds(0, count)]
        pltpu.make_async_copy(part, part, sem.at[c]).wait()

    own = quads(0)
    gather(0, RUNS[0][0], own)
    dispatch(0, RUNS[0][0])
    for copy in stay(send, recv, 0, 0):
        copy.start()

    def column_codes(source):
        rows = meta[...] if source == 0 else meta_near[source - 1]
        tall = jnp.concatenate([rows, jnp.zeros((TOK - 8, TOK), F32)], axis=0)
        colcode[source] = jnp.transpose(tall)

    column_codes(0)
    out_row = iota((256, 256), 0)
    in_row = ((out_row // 4) % 16) * 16 + (out_row // 64) * 4 + out_row % 4
    perm[0] = jnp.where(in_row == iota((256, 256), 1), 1.0, 0.0).astype(BF16)
    out_col = iota((256, 256), 1)
    in_col = ((out_col // 4) % 16) * 16 + (out_col // 64) * 4 + out_col % 4
    perm[1] = jnp.where(in_col == iota((256, 256), 0), 1.0, 0.0).astype(BF16)

    for load in loads[7:]:
        load.wait()
    for r in range(0, D, 256):
        win_t[:, r:r + 256] = jnp.transpose(win[r:r + 256, :])
        wout_t[:, r:r + 256] = jnp.transpose(wout[r:r + 256, :])
    for side in range(2):
        handed[side][0].wait_recv()
    column_codes(1)
    column_codes(2)
    quad = [own, quads(1), quads(2)]
    for part in (1, 2):
        for side in range(2):
            handed[side][part].wait_recv()
    for c in range(CHUNKS):
        for run in RUNS[c]:
            if run[2] > 0:
                gather(c, run, quad[run[2]])
                dispatch(c, run)
        if c > 0:
            for copy in stay(send, recv, 0, c):
                copy.start()

    for c in range(CHUNKS):
        await_all(recv, c, recv_sem)
        for copy in stay(send, recv, 0, c):
            copy.wait()
        base = c * SLOTS
        for g in range(2):
            packed = recv[c, g * 16:(g + 1) * 16].reshape(256, HALF)
            sorted_rows = dot(perm[0], packed, plain).astype(BF16)
            at = slice(base + g * 64, base + (g + 1) * 64)
            xrows[at, 0:HALF] = sorted_rows[0:64]
            xrows[at, HALF:] = sorted_rows[64:128]
            gorows[at, 0:HALF] = sorted_rows[128:192]
            gorows[at, HALF:] = sorted_rows[192:256]
        rows = slice(base, base + SLOTS)
        pre = dot(xrows[rows], win[...], plain)
        grad_act = dot(gorows[rows], wout_t[...], plain)
        act, slope = gelu_parts(pre)
        act = act.astype(BF16)
        actrows[rows] = act
        grad_pre = (grad_act * slope).astype(BF16)
        gprows[rows] = grad_pre
        score = jnp.sum(act.astype(F32) * grad_act, axis=1, keepdims=True)
        spread = jnp.where(iota((SLOTS, 128), 0) % CAP == iota((SLOTS, 128), 1), score, 0.0)
        high = spread.astype(BF16)
        low = (spread - high.astype(F32)).astype(BF16)
        group = jnp.where(
            iota((BLOCKS, SLOTS), 1) // CAP == iota((BLOCKS, SLOTS), 0), 1.0, 0.0
        ).astype(BF16)
        score_ret[c] = (dot(group, high, plain) + dot(group, low, plain)).reshape(BLOCKS, 1, 128)
        grad_rows = dot(grad_pre, win_t[...], plain).astype(BF16)
        for g in range(2):
            piece = grad_rows[g * 64:(g + 1) * 64]
            stack = jnp.concatenate([piece[:, q * 256:(q + 1) * 256] for q in range(4)], axis=0)
            mixed = dot(perm[1], stack, plain).astype(BF16)
            ret[c, g * 16:(g + 1) * 16] = mixed.reshape(16, 16, 256)

        for run in RUNS[c]:
            def give(b, carry, c=c, run=run):
                to = target(b, run[3], -1)
                pltpu.make_async_remote_copy(
                    ret.at[c, b], back.at[c, b], ret_sem.at[c], back_sem.at[c],
                    device_id=to, device_id_type=MESH,
                ).start()
                pltpu.make_async_remote_copy(
                    score_ret.at[c, b], score_back.at[c, b], sret_sem.at[c], sback_sem.at[c],
                    device_id=to, device_id_type=MESH,
                ).start()
                return carry

            each(c, run, give)
        for copy in stay(ret, back, 1, c) + stay(score_ret, score_back, 2, c):
            copy.start()

    theirs = pl.multiple_of((1 - rep) * HALF, HALF)
    mine = pl.multiple_of(rep * HALF, HALF)
    down = ((0,), (0,))
    wg_send[0] = dot(xrows[...], gprows[:, pl.ds(theirs, HALF)], down).astype(BF16)
    wg_send[1] = dot(actrows[...], gorows[:, pl.ds(theirs, HALF)], down).astype(BF16)
    swap = pltpu.make_async_remote_copy(
        wg_send, wg_recv, wgs_sem, wgr_sem, device_id=(1 - rep, me), device_id_type=MESH
    )
    swap.start()

    started = set()
    for c in range(CHUNKS):
        await_all(back, c, back_sem)
        for copy in stay(ret, back, 1, c):
            copy.wait()
        for lo, hi, source, _ in RUNS[c]:
            size = (hi - lo) * 16
            lane = iota((TOK, size), 1) + (c * BLOCKS + lo) * 16
            landed = back[c, lo:hi].reshape(size, 256)
            col0 = colcode[source, :, 0:1].astype(I32)
            col1 = colcode[source, :, 1:2].astype(I32)
            for q in range(4):
                pick = jnp.where(
                    lane == col0 + 4 * q, 1.0, jnp.where(lane == col1 + 4 * q, 1.0, 0.0)
                )
                piece = dot(pick.astype(BF16), landed, plain)
                where = slice(q * 256, (q + 1) * 256)
                if source in started:
                    piece = piece + total[source, :, where]
                if c == CHUNKS - 1:
                    part_send[source - 1, :, where] = piece.astype(BF16)
                else:
                    total[source, :, where] = piece
            started.add(source)
            if c == CHUNKS - 1:
                pltpu.make_async_remote_copy(
                    part_send.at[source - 1], part_recv.at[source - 1],
                    part_ssem.at[source - 1, 0], part_rsem.at[source - 1, 0],
                    device_id=near(2 - source), device_id_type=MESH,
                ).start()

    for c in range(CHUNKS):
        await_all(score_back, c, sback_sem)
        for copy in stay(score_ret, score_back, 2, c):
            copy.wait()
    scores = score_back[...].reshape(EXPERTS, 128)
    spot = iota((EXPERTS, TOK), 0)
    low_half = spot % BLOCKS < 16

    def score_rows(source):
        rows = meta[...] if source == 0 else meta_near[source - 1]
        if source == 0:
            here = spot < 16
        elif source == 1:
            here = ((spot >= BLOCKS) & low_half) | ((spot >= 16) & (spot < 24))
        else:
            here = ((spot >= BLOCKS) & jnp.logical_not(low_half)) | ((spot >= 24) & (spot < BLOCKS))
        found = []
        for k in range(2):
            code = rows[k:k + 1].astype(I32)
            hot = jnp.where((spot == code // 16) & here, 1.0, 0.0)
            got = jnp.zeros((1, TOK), F32)
            for s in range(CAP):
                hit = jnp.sum(hot * scores[:, s:s + 1], axis=0, keepdims=True)
                got = got + jnp.where(code % 16 == s, hit, 0.0)
            found.append(got)
        return jnp.concatenate(found + [jnp.zeros((6, TOK), F32)], axis=0)

    for source in (1, 2):
        score_send[source - 1] = score_rows(source)
        pltpu.make_async_remote_copy(
            score_send.at[source - 1], score_recv.at[source - 1],
            part_ssem.at[source - 1, 1], part_rsem.at[source - 1, 1],
            device_id=near(2 - source), device_id_type=MESH,
        ).start()
    own_scores = score_rows(0)

    own_in = dot(xrows[...], gprows[:, pl.ds(mine, HALF)], down)
    own_out = dot(actrows[...], gorows[:, pl.ds(mine, HALF)], down)
    swap.wait()
    gwin_ref[0] = (own_in + wg_recv[0].astype(F32)).astype(BF16)
    gwout_ref[0] = (own_out + wg_recv[1].astype(F32)).astype(BF16)

    for side in range(2):
        for kind, (sent, landed) in enumerate(((part_send, part_recv), (score_send, score_recv))):
            pltpu.make_async_remote_copy(
                sent.at[side], landed.at[side], part_ssem.at[side, kind], part_rsem.at[side, kind],
                device_id=near(1 - side), device_id_type=MESH,
            ).wait()
    gtok_ref[...] = (
        total[0] + part_recv[0].astype(F32) + part_recv[1].astype(F32)
    ).astype(BF16)
    all_scores = own_scores + score_recv[0] + score_recv[1]
    ggate_ref[...] = all_scores[0:2] / gate_low

    for side in range(2):
        for part in range(3):
            handed[side][part].wait_send()
    for c in range(CHUNKS):
        await_all(send, c, send_sem)
        await_all(ret, c, ret_sem)
        await_all(score_ret, c, sret_sem)


def finish(*refs):
    sources, results, sems = refs[:4], refs[4:8], refs[8]
    for i in range(4):
        pltpu.make_async_copy(sources[i], results[i], sems.at[i]).start()
    for i in range(4):
        pltpu.make_async_copy(sources[i], results[i], sems.at[i]).wait()


def body(tokens, cotangent, gate_values, expert_ids, keep_second, weight_in, weight_out):
    vmem = pl.BlockSpec(memory_space=pltpu.VMEM)
    hbm = pl.BlockSpec(memory_space=pl.ANY)
    dma = pltpu.SemaphoreType.DMA
    parts = pl.pallas_call(
        kernel,
        out_shape=(
            pltpu.VMEM((TOK, D), BF16),
            pltpu.VMEM((2, TOK), F32),
            pltpu.VMEM((1, D, HALF), BF16),
            pltpu.VMEM((1, F, HALF), BF16),
        ),
        in_specs=[hbm] * 7,
        out_specs=(vmem,) * 4,
        scratch_shapes=[
            pltpu.VMEM((D, F), BF16),
            pltpu.VMEM((F, D), BF16),
            pltpu.VMEM((F, D), BF16),
            pltpu.VMEM((D, F), BF16),
            pltpu.VMEM((2, TOK), F32),
            pltpu.VMEM((2, TOK), I32),
            pltpu.VMEM((1, TOK), I32),
            pltpu.VMEM((512, HALF), BF16),
            pltpu.VMEM((2, 512, HALF), BF16),
            pltpu.VMEM((8, TOK), F32),
            pltpu.VMEM((2, 8, TOK), F32),
            pltpu.VMEM((CHUNKS, BLOCKS, 16, HALF), BF16),
            pltpu.VMEM((CHUNKS, BLOCKS, 16, HALF), BF16),
            pltpu.VMEM((CHUNKS, BLOCKS, 16, 256), BF16),
            pltpu.VMEM((CHUNKS, BLOCKS, 16, 256), BF16),
            pltpu.VMEM((CHUNKS, BLOCKS, 1, 128), F32),
            pltpu.VMEM((CHUNKS, BLOCKS, 1, 128), F32),
            pltpu.VMEM((512, D), BF16),
            pltpu.VMEM((512, D), BF16),
            pltpu.VMEM((512, F), BF16),
            pltpu.VMEM((512, F), BF16),
            pltpu.VMEM((2, 256, 256), BF16),
            pltpu.VMEM((2, D, HALF), BF16),
            pltpu.VMEM((2, D, HALF), BF16),
            pltpu.VMEM((3, TOK, TOK), F32),
            pltpu.VMEM((3, TOK, D), F32),
            pltpu.VMEM((2, TOK, D), BF16),
            pltpu.VMEM((2, TOK, D), BF16),
            pltpu.VMEM((2, 8, TOK), F32),
            pltpu.VMEM((2, 8, TOK), F32),
            dma((9,)), dma((2, 3)), dma((2, 3)), dma((3, 3)),
            dma((CHUNKS,)), dma((CHUNKS,)), dma((CHUNKS,)), dma((CHUNKS,)),
            dma((CHUNKS,)), dma((CHUNKS,)), dma((2, 2)), dma((2, 2)), dma, dma,
        ],
        compiler_params=pltpu.CompilerParams(
            collective_id=0, has_side_effects=True, vmem_limit_bytes=60 * 2**20
        ),
        cost_estimate=pl.CostEstimate(
            flops=2 * 512 * 1024 * 1024 * 6, bytes_accessed=7 * 2**20, transcendentals=512 * 1024
        ),
    )(
        tokens,
        cotangent,
        gate_values.T,
        expert_ids.T,
        keep_second.reshape(1, TOK),
        weight_in,
        weight_out,
    )
    grad_tokens, grad_gates, grad_in, grad_out = pl.pallas_call(
        finish,
        out_shape=tuple(jax.ShapeDtypeStruct(p.shape, p.dtype) for p in parts),
        in_specs=[vmem] * 4,
        out_specs=(hbm,) * 4,
        scratch_shapes=[dma((4,))],
    )(*(pltpu.with_memory_space_constraint(p, pltpu.VMEM) for p in parts))
    return grad_tokens, grad_gates.T, grad_in, grad_out


def solution(mesh):
    in_specs = (
        P(("rep", "expert"), None),
        P(("rep", "expert"), None),
        P(("rep", "expert"), None),
        P(("rep", "expert"), None),
        P(("rep", "expert")),
        P("expert", None, None),
        P("expert", None, None),
    )
    out_specs = (
        P(("rep", "expert"), None),
        P(("rep", "expert"), None),
        P("expert", None, "rep"),
        P("expert", None, "rep"),
    )
    return jax.shard_map(body, mesh=mesh, in_specs=in_specs, out_specs=out_specs, check_vma=False)
```

time: 96.4 us -> 83.2 us (0.86); the launches traced: 95 us -> 83.1 us
  local copies, waits for them, and re-layouts: 6.23 us -> 0 us
  Pallas kernels: 88.1 us -> 82.3 us
    unnamed x6 -> x0, local copies, waits for them, and re-layouts: 6.23 us -> none
    pallas_call x1 -> x2, Pallas kernels: 88.1 us -> 82.3 us  [the longest x1 80.9 us: body(): pl.pallas_call(kernel, out_shape=(pltpu.VMEM((TOK, D), BF16), pltpu.VMEM(...]
where the time goes in v2:
time: 83.2 us; the launch traced here: 83.1 us
  Pallas kernels  82.3 us (99%)
    pallas_call x1, Pallas kernels, body(): pl.pallas_call(kernel, out_shape=(pltpu.VMEM((TOK, D), BF16), pltpu.VMEM(...  80.9 us

profile of v2, /device:TPU:2, one launch (start us, length us, event | category | flops | bytes accessed | tf_op | source)
XLA Modules:
  0.0 83.1 jit_solution(289206461935981346)
XLA Ops:
  0.6 80.9 %shard_map.102 = (bf16[128,1024]{1,0:T(8,128)(2,1)S(1)}, f32[2,128]{1,0:T(2,128)S(1)}, bf16[1,1024,512]{2,1,0:T(8,128)(2,1)S(1)}, bf16[1,1024,512]{2,1,0:T(8,128)(2,1)S(1)}) custom-call(bf16[128,1024]{1,0:T(8,128)(2,1)} %tokens_hbm.1, bf16[128,1024]{1,0:T(8,128)(2,1)} %cot_hbm.1, f32[2,128]{1,0:T(2,128)} %bitcast.4, s32[2,128]{1,0:T(2,128)} %bitcast.5, ...), custom_call_target="tpu_custom_call" | custom-call | flops 6442450944 | bytes 7340032 | tf_op jit(solution)/shard_map/pallas_call | solution.py:418
  81.5 1.4 %shard_map.103 = (bf16[128,1024]{1,0:T(8,128)(2,1)}, f32[2,128]{1,0:T(2,128)}, bf16[1,1024,512]{2,1,0:T(8,128)(2,1)}, bf16[1,1024,512]{2,1,0:T(8,128)(2,1)}) custom-call(bf16[128,1024]{1,0:T(8,128)(2,1)S(1)} %get-tuple-element.12.refs_0_, f32[2,128]{1,0:T(2,128)S(1)} %get-tuple-element.13.refs_1_, bf16[1,1024,512]{2,1,0:T(8,128)(2,1)S(1)} %get-tuple-element.14.refs_2_, ...), custom_call_target="tpu_custom_call" | custom-call | tf_op jit(solution)/shard_map/pallas_call | solution.py:478

commit v3 on v2

--- a/solution.py
+++ b/solution.py
@@ -17,6 +17,7 @@
 D = 1024
 F = 1024
 HALF = 512
+QUARTER = 256
 ORDER = (0, 4, 3, 5, 2, 6, 1, 7)
 CHUNKS = 4
 BLOCKS = EXPERTS // CHUNKS
@@ -28,6 +29,7 @@
     ((0, 16, 1, 1), (16, 32, 2, -1)),
     ((0, 16, 1, 0), (16, 32, 2, 0)),
 )
+FIRST = (0, 1, 2, 3)
 STAY = ((0, 0), (3, 0), (3, 16))
 
 
@@ -56,7 +58,7 @@
     win, wout, win_t, wout_t, gates, ids_in, keep, xcat, xnear, meta, meta_near, send, recv, ret, back,
     score_ret, score_back, xrows, gorows, actrows, gprows, perm, wg_send, wg_recv,
     colcode, total, part_send, part_recv, score_send, score_recv,
-    load_sem, near_send, near_recv, stay_sem, send_sem, recv_sem, ret_sem, back_sem,
+    met_sem, load_sem, near_send, near_recv, stay_sem, send_sem, recv_sem, ret_sem, back_sem,
     sret_sem, sback_sem, part_ssem, part_rsem, wgs_sem, wgr_sem,
 ):
     me = lax.axis_index("expert")
@@ -78,28 +80,56 @@
         pltpu.make_async_copy(ids_hbm, ids_in, load_sem.at[0]),
         pltpu.make_async_copy(gates_hbm, gates, load_sem.at[1]),
         pltpu.make_async_copy(keep_hbm, keep, load_sem.at[2]),
-        pltpu.make_async_copy(tokens_hbm.at[:, 0:HALF], xcat.at[0:128], load_sem.at[3]),
-        pltpu.make_async_copy(tokens_hbm.at[:, HALF:D], xcat.at[128:256], load_sem.at[4]),
-        pltpu.make_async_copy(cot_hbm.at[:, 0:HALF], xcat.at[256:384], load_sem.at[5]),
-        pltpu.make_async_copy(cot_hbm.at[:, HALF:D], xcat.at[384:512], load_sem.at[6]),
-        pltpu.make_async_copy(win_hbm.at[0], win, load_sem.at[7]),
-        pltpu.make_async_copy(wout_hbm.at[0], wout, load_sem.at[8]),
+        pltpu.make_async_copy(win_hbm.at[0], win, load_sem.at[3]),
+        pltpu.make_async_copy(wout_hbm.at[0], wout, load_sem.at[4]),
     ]
-    for load in loads[:7]:
+    row_loads = [
+        [
+            pltpu.make_async_copy(
+                held.at[:, q * QUARTER:(q + 1) * QUARTER],
+                xcat.at[kind, q * TOK:(q + 1) * TOK],
+                load_sem.at[5 + 4 * kind + q],
+            )
+            for q in range(4)
+        ]
+        for kind, held in enumerate((tokens_hbm, cot_hbm))
+    ]
+    for load in row_loads[0] + loads[:3] + row_loads[1]:
         load.start()
 
     bar = pltpu.get_barrier_semaphore()
 
-    def greet(i, carry):
-        to = device(i // PLANE - 3, (i // NX) % NY, i % NX)
+    beside = [[device(*(step * (axis == a) for a in range(3))) for step in (1, -1)] for axis in range(3)]
+    for to in [to for pair in beside for to in pair] + [(1 - rep, me)]:
         pl.semaphore_signal(bar, inc=1, device_id=to, device_id_type=MESH)
-        return carry
-
-    lax.fori_loop(0, 3 * PLANE, greet, 0)
-    lax.fori_loop(3 * PLANE + 1, 7 * PLANE, greet, 0)
-    pl.semaphore_signal(bar, inc=1, device_id=(1 - rep, me), device_id_type=MESH)
-    for load in loads[7:]:
+    for load in loads[3:]:
         load.start()
+
+    def know(axis, at):
+        for to in beside[axis]:
+            pl.semaphore_signal(met_sem.at[at], inc=1, device_id=to, device_id_type=MESH)
+        pl.semaphore_wait(met_sem.at[at], 2)
+
+    def hand_over(side):
+        to = near(side)
+        return [
+            pltpu.make_async_remote_copy(
+                meta, meta_near.at[side], near_send.at[side, 2], near_recv.at[side, 2],
+                device_id=to, device_id_type=MESH,
+            ) if kind == 2 else pltpu.make_async_remote_copy(
+                xcat.at[kind], xnear.at[side, kind],
+                near_send.at[side, kind], near_recv.at[side, kind],
+                device_id=to, device_id_type=MESH,
+            )
+            for kind in range(3)
+        ]
+
+    handed = [hand_over(0), hand_over(1)]
+    for load in row_loads[0]:
+        load.wait()
+    pl.semaphore_wait(bar, 7)
+    for side in range(2):
+        handed[side][0].start()
 
     for load in loads[:3]:
         load.wait()
@@ -132,49 +162,31 @@
         axis=0,
     )
 
-    def hand_over(side):
-        to = near(side)
-        return [
-            pltpu.make_async_remote_copy(
-                meta, meta_near.at[side], near_send.at[side, 0], near_recv.at[side, 0],
-                device_id=to, device_id_type=MESH,
-            )
-        ] + [
-            pltpu.make_async_remote_copy(
-                xcat.at[part * 256:(part + 1) * 256],
-                xnear.at[side, part * 256:(part + 1) * 256],
-                near_send.at[side, 1 + part], near_recv.at[side, 1 + part],
-                device_id=to, device_id_type=MESH,
-            )
-            for part in range(2)
-        ]
-
-    handed = [hand_over(0), hand_over(1)]
-    for load in loads[3:7]:
+    for side in range(2):
+        handed[side][2].start()
+    for load in row_loads[1]:
         load.wait()
-    pl.semaphore_wait(bar, 7 * PLANE)
-    for part in range(3):
-        for side in range(2):
-            handed[side][part].start()
+    for side in range(2):
+        handed[side][1].start()
 
     def quads(source):
         rows = meta[...] if source == 0 else meta_near[source - 1]
         code0, code1 = rows[0:1].astype(I32), rows[1:2].astype(I32)
-        one = jnp.ones((1, TOK), F32)
         return (
             jnp.concatenate([code0 + 4 * q for q in range(4)], axis=1),
             jnp.concatenate([code1 + 4 * q for q in range(4)], axis=1),
-            jnp.concatenate([one, one, rows[2:3], rows[2:3]], axis=1),
-            jnp.concatenate([one, one, rows[3:4], rows[3:4]], axis=1),
+            jnp.concatenate([rows[2:3]] * 4, axis=1),
+            jnp.concatenate([rows[3:4]] * 4, axis=1),
         )
 
-    def gather(c, run, quad):
+    def gather(kind, c, run, quad):
         lo, hi, source, _ = run
         row = iota(((hi - lo) * 16, 512), 0) + (c * BLOCKS + lo) * 16
-        pick = jnp.where(row == quad[0], quad[2], jnp.where(row == quad[1], quad[3], 0.0))
-        held = xcat[...] if source == 0 else xnear[source - 1]
+        one, two = (1.0, 1.0) if kind == 0 else quad[2:]
+        pick = jnp.where(row == quad[0], one, jnp.where(row == quad[1], two, 0.0))
+        held = xcat[kind] if source == 0 else xnear[source - 1, kind]
         block = dot(pick.astype(BF16), held, plain).astype(BF16)
-        send[c, lo:hi] = block.reshape(hi - lo, 16, HALF)
+        send[kind, c, lo:hi] = block.reshape(hi - lo, 16, QUARTER)
 
     def target(b, off, sign):
         return device(sign * off, sign * ((b // NX) % NY), sign * (b % NX))
@@ -183,10 +195,11 @@
         lo, hi = run[:2]
         lax.fori_loop(lo + ((c, lo) in STAY), hi, step, 0)
 
-    def dispatch(c, run):
+    def dispatch(kind, c, run):
         def go(b, carry):
             pltpu.make_async_remote_copy(
-                send.at[c, b], recv.at[c, b], send_sem.at[c], recv_sem.at[c],
+                send.at[kind, c, b], recv.at[kind, c, b],
+                send_sem.at[kind, c], recv_sem.at[kind, c],
                 device_id=target(b, run[3], 1), device_id_type=MESH,
             ).start()
             return carry
@@ -205,11 +218,18 @@
         part = buffer.at[c, pl.ds(0, count)]
         pltpu.make_async_copy(part, part, sem.at[c]).wait()
 
+    def stay_rows(kind, c):
+        return stay(send.at[kind], recv.at[kind], kind, c)
+
+    know(2, 0)
+    know(1, 1)
+    know(1, 2)
     own = quads(0)
-    gather(0, RUNS[0][0], own)
-    dispatch(0, RUNS[0][0])
-    for copy in stay(send, recv, 0, 0):
-        copy.start()
+    for kind in range(2):
+        gather(kind, 0, RUNS[0][0], own)
+        dispatch(kind, 0, RUNS[0][0])
+        for copy in stay_rows(kind, 0):
+            copy.start()
 
     def column_codes(source):
         rows = meta[...] if source == 0 else meta_near[source - 1]
@@ -224,41 +244,43 @@
     in_col = ((out_col // 4) % 16) * 16 + (out_col // 64) * 4 + out_col % 4
     perm[1] = jnp.where(in_col == iota((256, 256), 0), 1.0, 0.0).astype(BF16)
 
-    for load in loads[7:]:
+    know(0, 3)
+    know(0, 4)
+    know(0, 5)
+    for load in loads[3:]:
         load.wait()
     for r in range(0, D, 256):
         win_t[:, r:r + 256] = jnp.transpose(win[r:r + 256, :])
         wout_t[:, r:r + 256] = jnp.transpose(wout[r:r + 256, :])
     for side in range(2):
-        handed[side][0].wait_recv()
+        handed[side][2].wait_recv()
     column_codes(1)
     column_codes(2)
     quad = [own, quads(1), quads(2)]
-    for part in (1, 2):
+    for kind, order in ((0, FIRST), (1, range(CHUNKS))):
         for side in range(2):
-            handed[side][part].wait_recv()
+            handed[side][kind].wait_recv()
+        for c in order:
+            for run in RUNS[c]:
+                if run[2] > 0:
+                    gather(kind, c, run, quad[run[2]])
+                    dispatch(kind, c, run)
+            if c > 0:
+                for copy in stay_rows(kind, c):
+                    copy.start()
+
     for c in range(CHUNKS):
-        for run in RUNS[c]:
-            if run[2] > 0:
-                gather(c, run, quad[run[2]])
-                dispatch(c, run)
-        if c > 0:
-            for copy in stay(send, recv, 0, c):
-                copy.start()
-
-    for c in range(CHUNKS):
-        await_all(recv, c, recv_sem)
-        for copy in stay(send, recv, 0, c):
-            copy.wait()
         base = c * SLOTS
-        for g in range(2):
-            packed = recv[c, g * 16:(g + 1) * 16].reshape(256, HALF)
-            sorted_rows = dot(perm[0], packed, plain).astype(BF16)
-            at = slice(base + g * 64, base + (g + 1) * 64)
-            xrows[at, 0:HALF] = sorted_rows[0:64]
-            xrows[at, HALF:] = sorted_rows[64:128]
-            gorows[at, 0:HALF] = sorted_rows[128:192]
-            gorows[at, HALF:] = sorted_rows[192:256]
+        for kind, plain_rows in enumerate((xrows, gorows)):
+            await_all(recv.at[kind], c, recv_sem.at[kind])
+            for copy in stay_rows(kind, c):
+                copy.wait()
+            for g in range(2):
+                packed = recv[kind, c, g * 16:(g + 1) * 16].reshape(256, QUARTER)
+                sorted_rows = dot(perm[0], packed, plain).astype(BF16)
+                at = slice(base + g * 64, base + (g + 1) * 64)
+                for q in range(4):
+                    plain_rows[at, q * QUARTER:(q + 1) * QUARTER] = sorted_rows[q * 64:(q + 1) * 64]
         rows = slice(base, base + SLOTS)
         pre = dot(xrows[rows], win[...], plain)
         grad_act = dot(gorows[rows], wout_t[...], plain)
@@ -296,7 +318,7 @@
                 return carry
 
             each(c, run, give)
-        for copy in stay(ret, back, 1, c) + stay(score_ret, score_back, 2, c):
+        for copy in stay(ret, back, 2, c) + stay(score_ret, score_back, 3, c):
             copy.start()
 
     theirs = pl.multiple_of((1 - rep) * HALF, HALF)
@@ -312,7 +334,7 @@
     started = set()
     for c in range(CHUNKS):
         await_all(back, c, back_sem)
-        for copy in stay(ret, back, 1, c):
+        for copy in stay(ret, back, 2, c):
             copy.wait()
         for lo, hi, source, _ in RUNS[c]:
             size = (hi - lo) * 16
@@ -342,7 +364,7 @@
 
     for c in range(CHUNKS):
         await_all(score_back, c, sback_sem)
-        for copy in stay(score_ret, score_back, 2, c):
+        for copy in stay(score_ret, score_back, 3, c):
             copy.wait()
     scores = score_back[...].reshape(EXPERTS, 128)
     spot = iota((EXPERTS, TOK), 0)
@@ -398,7 +420,8 @@
         for part in range(3):
             handed[side][part].wait_send()
     for c in range(CHUNKS):
-        await_all(send, c, send_sem)
+        for kind in range(2):
+            await_all(send.at[kind], c, send_sem.at[kind])
         await_all(ret, c, ret_sem)
         await_all(score_ret, c, sret_sem)
 
@@ -433,12 +456,12 @@
             pltpu.VMEM((2, TOK), F32),
             pltpu.VMEM((2, TOK), I32),
             pltpu.VMEM((1, TOK), I32),
-            pltpu.VMEM((512, HALF), BF16),
-            pltpu.VMEM((2, 512, HALF), BF16),
+            pltpu.VMEM((2, 512, QUARTER), BF16),
+            pltpu.VMEM((2, 2, 512, QUARTER), BF16),
             pltpu.VMEM((8, TOK), F32),
             pltpu.VMEM((2, 8, TOK), F32),
-            pltpu.VMEM((CHUNKS, BLOCKS, 16, HALF), BF16),
-            pltpu.VMEM((CHUNKS, BLOCKS, 16, HALF), BF16),
+            pltpu.VMEM((2, CHUNKS, BLOCKS, 16, QUARTER), BF16),
+            pltpu.VMEM((2, CHUNKS, BLOCKS, 16, QUARTER), BF16),
             pltpu.VMEM((CHUNKS, BLOCKS, 16, 256), BF16),
             pltpu.VMEM((CHUNKS, BLOCKS, 16, 256), BF16),
             pltpu.VMEM((CHUNKS, BLOCKS, 1, 128), F32),
@@ -456,8 +479,9 @@
             pltpu.VMEM((2, TOK, D), BF16),
             pltpu.VMEM((2, 8, TOK), F32),
             pltpu.VMEM((2, 8, TOK), F32),
-            dma((9,)), dma((2, 3)), dma((2, 3)), dma((3, 3)),
-            dma((CHUNKS,)), dma((CHUNKS,)), dma((CHUNKS,)), dma((CHUNKS,)),
+            pltpu.SemaphoreType.REGULAR((6,)),
+            dma((13,)), dma((2, 3)), dma((2, 3)), dma((4, 3)),
+            dma((2, CHUNKS)), dma((2, CHUNKS)), dma((CHUNKS,)), dma((CHUNKS,)),
             dma((CHUNKS,)), dma((CHUNKS,)), dma((2, 2)), dma((2, 2)), dma, dma,
         ],
         compiler_params=pltpu.CompilerParams(

time: 83.2 us -> 74.4 us (0.89)
  Pallas kernels: 82.3 us -> 73.5 us
    pallas_call x1, Pallas kernels: 80.9 us -> 72.1 us  [body(): pl.pallas_call(kernel, out_shape=(pltpu.VMEM((TOK, D), BF16), pltpu.VMEM(...]
where the time goes in v3:
time: 74.4 us; the launch traced here: 74.3 us
  Pallas kernels  73.5 us (99%)
  between operations  0.8 us (1%)
    pallas_call x1, Pallas kernels, body(): pl.pallas_call(kernel, out_shape=(pltpu.VMEM((TOK, D), BF16), pltpu.VMEM(...  72.1 us

profile of v3, /device:TPU:2, one launch (start us, length us, event | category | flops | bytes accessed | tf_op | source)
XLA Modules:
  0.0 74.3 jit_solution(3093998411890773685)
XLA Ops:
  0.6 72.1 %shard_map.102 = (bf16[128,1024]{1,0:T(8,128)(2,1)S(1)}, f32[2,128]{1,0:T(2,128)S(1)}, bf16[1,1024,512]{2,1,0:T(8,128)(2,1)S(1)}, bf16[1,1024,512]{2,1,0:T(8,128)(2,1)S(1)}) custom-call(bf16[128,1024]{1,0:T(8,128)(2,1)} %tokens_hbm.1, bf16[128,1024]{1,0:T(8,128)(2,1)} %cot_hbm.1, f32[2,128]{1,0:T(2,128)} %bitcast.4, s32[2,128]{1,0:T(2,128)} %bitcast.5, ...), custom_call_target="tpu_custom_call" | custom-call | flops 6442450944 | bytes 7340032 | tf_op jit(solution)/shard_map/pallas_call | solution.py:441
  72.7 1.4 %shard_map.103 = (bf16[128,1024]{1,0:T(8,128)(2,1)}, f32[2,128]{1,0:T(2,128)}, bf16[1,1024,512]{2,1,0:T(8,128)(2,1)}, bf16[1,1024,512]{2,1,0:T(8,128)(2,1)}) custom-call(bf16[128,1024]{1,0:T(8,128)(2,1)S(1)} %get-tuple-element.12.refs_0_, f32[2,128]{1,0:T(2,128)S(1)} %get-tuple-element.13.refs_1_, bf16[1,1024,512]{2,1,0:T(8,128)(2,1)S(1)} %get-tuple-element.14.refs_2_, ...), custom_call_target="tpu_custom_call" | custom-call | tf_op jit(solution)/shard_map/pallas_call | solution.py:502

commit v4 on v3

--- a/solution.py
+++ b/solution.py
@@ -29,7 +29,8 @@
     ((0, 16, 1, 1), (16, 32, 2, -1)),
     ((0, 16, 1, 0), (16, 32, 2, 0)),
 )
-FIRST = (0, 1, 2, 3)
+LEAVE = ((0, 1, 2, 3), (0, 1, 2, 3))
+WORK = (3, 0, 1, 2)
 STAY = ((0, 0), (3, 0), (3, 16))
 
 
@@ -56,7 +57,7 @@
     tokens_hbm, cot_hbm, gates_hbm, ids_hbm, keep_hbm, win_hbm, wout_hbm,
     gtok_ref, ggate_ref, gwin_ref, gwout_ref,
     win, wout, win_t, wout_t, gates, ids_in, keep, xcat, xnear, meta, meta_near, send, recv, ret, back,
-    score_ret, score_back, xrows, gorows, actrows, gprows, perm, wg_send, wg_recv,
+    score_ret, score_back, xrows, gorows, actrows, gprows, slopes, perm, wg_send, wg_recv,
     colcode, total, part_send, part_recv, score_send, score_recv,
     met_sem, load_sem, near_send, near_recv, stay_sem, send_sem, recv_sem, ret_sem, back_sem,
     sret_sem, sback_sem, part_ssem, part_rsem, wgs_sem, wgr_sem,
@@ -188,23 +189,40 @@
         block = dot(pick.astype(BF16), held, plain).astype(BF16)
         send[kind, c, lo:hi] = block.reshape(hi - lo, 16, QUARTER)
 
-    def target(b, off, sign):
-        return device(sign * off, sign * ((b // NX) % NY), sign * (b % NX))
-
-    def each(c, run, step):
-        lo, hi = run[:2]
-        lax.fori_loop(lo + ((c, lo) in STAY), hi, step, 0)
+    along_x = {
+        sign: [lax.rem(my_x + (sign * dx) % NX, NX) for dx in range(NX)] for sign in (1, -1)
+    }
+
+    def each(c, run, sign, step):
+        lo, hi, _, off = run
+        plane = lax.rem(my_z + (sign * off) % NZ, NZ) * PLANE
+        rows = lo // NX
+
+        def four(row, skip):
+            dy = lax.rem(row, NY)
+            line = plane + lax.rem(my_y + (dy if sign == 1 else NY - dy), NY) * NX
+            for dx in range(skip, NX):
+                step(row * NX + dx, (rep, line + along_x[sign][dx]))
+
+        if (c, lo) in STAY:
+            four(rows, 1)
+            rows += 1
+
+        def turn(row, carry):
+            four(row, 0)
+            return carry
+
+        lax.fori_loop(rows, hi // NX, turn, 0)
 
     def dispatch(kind, c, run):
-        def go(b, carry):
+        def go(b, to):
             pltpu.make_async_remote_copy(
                 send.at[kind, c, b], recv.at[kind, c, b],
                 send_sem.at[kind, c], recv_sem.at[kind, c],
-                device_id=target(b, run[3], 1), device_id_type=MESH,
+                device_id=to, device_id_type=MESH,
             ).start()
-            return carry
-
-        each(c, run, go)
+
+        each(c, run, 1, go)
 
     def stay(sources, results, kind, c):
         return [
@@ -257,7 +275,7 @@
     column_codes(1)
     column_codes(2)
     quad = [own, quads(1), quads(2)]
-    for kind, order in ((0, FIRST), (1, range(CHUNKS))):
+    for kind, order in enumerate(LEAVE):
         for side in range(2):
             handed[side][kind].wait_recv()
         for c in order:
@@ -269,25 +287,30 @@
                 for copy in stay_rows(kind, c):
                     copy.start()
 
-    for c in range(CHUNKS):
-        base = c * SLOTS
-        for kind, plain_rows in enumerate((xrows, gorows)):
-            await_all(recv.at[kind], c, recv_sem.at[kind])
-            for copy in stay_rows(kind, c):
-                copy.wait()
-            for g in range(2):
-                packed = recv[kind, c, g * 16:(g + 1) * 16].reshape(256, QUARTER)
-                sorted_rows = dot(perm[0], packed, plain).astype(BF16)
-                at = slice(base + g * 64, base + (g + 1) * 64)
-                for q in range(4):
-                    plain_rows[at, q * QUARTER:(q + 1) * QUARTER] = sorted_rows[q * 64:(q + 1) * 64]
-        rows = slice(base, base + SLOTS)
-        pre = dot(xrows[rows], win[...], plain)
+    def settle(kind, c, plain_rows):
+        await_all(recv.at[kind], c, recv_sem.at[kind])
+        for copy in stay_rows(kind, c):
+            copy.wait()
+        for g in range(2):
+            packed = recv[kind, c, g * 16:(g + 1) * 16].reshape(256, QUARTER)
+            sorted_rows = dot(perm[0], packed, plain).astype(BF16)
+            at = slice(c * SLOTS + g * 64, c * SLOTS + (g + 1) * 64)
+            for q in range(4):
+                plain_rows[at, q * QUARTER:(q + 1) * QUARTER] = sorted_rows[q * 64:(q + 1) * 64]
+
+    for c in WORK:
+        settle(0, c, xrows)
+        rows = slice(c * SLOTS, (c + 1) * SLOTS)
+        act, slope = gelu_parts(dot(xrows[rows], win[...], plain))
+        actrows[rows] = act.astype(BF16)
+        slopes[rows] = slope
+
+    for c in WORK:
+        settle(1, c, gorows)
+        rows = slice(c * SLOTS, (c + 1) * SLOTS)
         grad_act = dot(gorows[rows], wout_t[...], plain)
-        act, slope = gelu_parts(pre)
-        act = act.astype(BF16)
-        actrows[rows] = act
-        grad_pre = (grad_act * slope).astype(BF16)
+        act = actrows[rows]
+        grad_pre = (grad_act * slopes[rows]).astype(BF16)
         gprows[rows] = grad_pre
         score = jnp.sum(act.astype(F32) * grad_act, axis=1, keepdims=True)
         spread = jnp.where(iota((SLOTS, 128), 0) % CAP == iota((SLOTS, 128), 1), score, 0.0)
@@ -305,8 +328,7 @@
             ret[c, g * 16:(g + 1) * 16] = mixed.reshape(16, 16, 256)
 
         for run in RUNS[c]:
-            def give(b, carry, c=c, run=run):
-                to = target(b, run[3], -1)
+            def give(b, to, c=c):
                 pltpu.make_async_remote_copy(
                     ret.at[c, b], back.at[c, b], ret_sem.at[c], back_sem.at[c],
                     device_id=to, device_id_type=MESH,
@@ -315,9 +337,8 @@
                     score_ret.at[c, b], score_back.at[c, b], sret_sem.at[c], sback_sem.at[c],
                     device_id=to, device_id_type=MESH,
                 ).start()
-                return carry
-
-            each(c, run, give)
+
+            each(c, run, -1, give)
         for copy in stay(ret, back, 2, c) + stay(score_ret, score_back, 3, c):
             copy.start()
 
@@ -332,7 +353,7 @@
     swap.start()
 
     started = set()
-    for c in range(CHUNKS):
+    for c in WORK:
         await_all(back, c, back_sem)
         for copy in stay(ret, back, 2, c):
             copy.wait()
@@ -350,12 +371,12 @@
                 where = slice(q * 256, (q + 1) * 256)
                 if source in started:
                     piece = piece + total[source, :, where]
-                if c == CHUNKS - 1:
+                if c == WORK[-1] and source > 0:
                     part_send[source - 1, :, where] = piece.astype(BF16)
                 else:
                     total[source, :, where] = piece
             started.add(source)
-            if c == CHUNKS - 1:
+            if c == WORK[-1] and source > 0:
                 pltpu.make_async_remote_copy(
                     part_send.at[source - 1], part_recv.at[source - 1],
                     part_ssem.at[source - 1, 0], part_rsem.at[source - 1, 0],
@@ -470,6 +491,7 @@
             pltpu.VMEM((512, D), BF16),
             pltpu.VMEM((512, F), BF16),
             pltpu.VMEM((512, F), BF16),
+            pltpu.VMEM((512, F), F32),
             pltpu.VMEM((2, 256, 256), BF16),
             pltpu.VMEM((2, D, HALF), BF16),
             pltpu.VMEM((2, D, HALF), BF16),

time: 74.4 us -> 73.2 us (0.984)
  Pallas kernels: 73.5 us -> 72.1 us
    pallas_call x1, Pallas kernels: 72.1 us -> 70.6 us  [body(): pl.pallas_call(kernel, out_shape=(pltpu.VMEM((TOK, D), BF16), pltpu.VMEM(...]
where the time goes in v4:
time: 73.2 us; the launch traced here: 72.9 us
  Pallas kernels  72.1 us (98%)
  between operations  0.8 us (1%)
    pallas_call x1, Pallas kernels, body(): pl.pallas_call(kernel, out_shape=(pltpu.VMEM((TOK, D), BF16), pltpu.VMEM(...  70.6 us

profile of v4, /device:TPU:2, one launch (start us, length us, event | category | flops | bytes accessed | tf_op | source)
XLA Modules:
  0.0 72.9 jit_solution(15333266264335788601)
XLA Ops:
  0.6 70.6 %shard_map.102 = (bf16[128,1024]{1,0:T(8,128)(2,1)S(1)}, f32[2,128]{1,0:T(2,128)S(1)}, bf16[1,1024,512]{2,1,0:T(8,128)(2,1)S(1)}, bf16[1,1024,512]{2,1,0:T(8,128)(2,1)S(1)}) custom-call(bf16[128,1024]{1,0:T(8,128)(2,1)} %tokens_hbm.1, bf16[128,1024]{1,0:T(8,128)(2,1)} %cot_hbm.1, f32[2,128]{1,0:T(2,128)} %bitcast.4, s32[2,128]{1,0:T(2,128)} %bitcast.5, ...), custom_call_target="tpu_custom_call" | custom-call | flops 6442450944 | bytes 7340032 | tf_op jit(solution)/shard_map/pallas_call | solution.py:462
  71.3 1.4 %shard_map.103 = (bf16[128,1024]{1,0:T(8,128)(2,1)}, f32[2,128]{1,0:T(2,128)}, bf16[1,1024,512]{2,1,0:T(8,128)(2,1)}, bf16[1,1024,512]{2,1,0:T(8,128)(2,1)}) custom-call(bf16[128,1024]{1,0:T(8,128)(2,1)S(1)} %get-tuple-element.12.refs_0_, f32[2,128]{1,0:T(2,128)S(1)} %get-tuple-element.13.refs_1_, bf16[1,1024,512]{2,1,0:T(8,128)(2,1)S(1)} %get-tuple-element.14.refs_2_, ...), custom_call_target="tpu_custom_call" | custom-call | tf_op jit(solution)/shard_map/pallas_call | solution.py:524

commit v5 on v4

--- a/solution.py
+++ b/solution.py
@@ -352,36 +352,49 @@
     )
     swap.start()
 
+    def hand_back(source, q):
+        side, where = source - 1, slice(q * QUARTER, (q + 1) * QUARTER)
+        return pltpu.make_async_remote_copy(
+            part_send.at[side, :, where], part_recv.at[side, :, where],
+            part_ssem.at[side, q], part_rsem.at[side, q],
+            device_id=near(2 - source), device_id_type=MESH,
+        )
+
+    def picks_of(c, run):
+        lo, hi, source, _ = run
+        lane = iota((TOK, (hi - lo) * 16), 1) + (c * BLOCKS + lo) * 16
+        col0 = colcode[source, :, 0:1].astype(I32)
+        col1 = colcode[source, :, 1:2].astype(I32)
+        return [
+            jnp.where(
+                lane == col0 + 4 * q, 1.0, jnp.where(lane == col1 + 4 * q, 1.0, 0.0)
+            ).astype(BF16)
+            for q in range(4)
+        ]
+
     started = set()
     for c in WORK:
+        last = c == WORK[-1]
+        if last:
+            own_in = dot(xrows[...], gprows[:, pl.ds(mine, HALF)], down)
+            own_out = dot(actrows[...], gorows[:, pl.ds(mine, HALF)], down)
+        picks = [picks_of(c, run) for run in RUNS[c]]
         await_all(back, c, back_sem)
         for copy in stay(ret, back, 2, c):
             copy.wait()
-        for lo, hi, source, _ in RUNS[c]:
-            size = (hi - lo) * 16
-            lane = iota((TOK, size), 1) + (c * BLOCKS + lo) * 16
-            landed = back[c, lo:hi].reshape(size, 256)
-            col0 = colcode[source, :, 0:1].astype(I32)
-            col1 = colcode[source, :, 1:2].astype(I32)
-            for q in range(4):
-                pick = jnp.where(
-                    lane == col0 + 4 * q, 1.0, jnp.where(lane == col1 + 4 * q, 1.0, 0.0)
-                )
-                piece = dot(pick.astype(BF16), landed, plain)
-                where = slice(q * 256, (q + 1) * 256)
+        for q in range(4):
+            where = slice(q * QUARTER, (q + 1) * QUARTER)
+            for pick, (lo, hi, source, _) in zip(picks, RUNS[c]):
+                landed = back[c, lo:hi].reshape((hi - lo) * 16, QUARTER)
+                piece = dot(pick[q], landed, plain)
                 if source in started:
                     piece = piece + total[source, :, where]
-                if c == WORK[-1] and source > 0:
+                if last and source > 0:
                     part_send[source - 1, :, where] = piece.astype(BF16)
+                    hand_back(source, q).start()
                 else:
                     total[source, :, where] = piece
-            started.add(source)
-            if c == WORK[-1] and source > 0:
-                pltpu.make_async_remote_copy(
-                    part_send.at[source - 1], part_recv.at[source - 1],
-                    part_ssem.at[source - 1, 0], part_rsem.at[source - 1, 0],
-                    device_id=near(2 - source), device_id_type=MESH,
-                ).start()
+        started.update(run[2] for run in RUNS[c])
 
     for c in range(CHUNKS):
         await_all(score_back, c, sback_sem)
@@ -414,23 +427,23 @@
         score_send[source - 1] = score_rows(source)
         pltpu.make_async_remote_copy(
             score_send.at[source - 1], score_recv.at[source - 1],
-            part_ssem.at[source - 1, 1], part_rsem.at[source - 1, 1],
+            part_ssem.at[source - 1, 4], part_rsem.at[source - 1, 4],
             device_id=near(2 - source), device_id_type=MESH,
         ).start()
     own_scores = score_rows(0)
 
-    own_in = dot(xrows[...], gprows[:, pl.ds(mine, HALF)], down)
-    own_out = dot(actrows[...], gorows[:, pl.ds(mine, HALF)], down)
     swap.wait()
     gwin_ref[0] = (own_in + wg_recv[0].astype(F32)).astype(BF16)
     gwout_ref[0] = (own_out + wg_recv[1].astype(F32)).astype(BF16)
 
-    for side in range(2):
-        for kind, (sent, landed) in enumerate(((part_send, part_recv), (score_send, score_recv))):
-            pltpu.make_async_remote_copy(
-                sent.at[side], landed.at[side], part_ssem.at[side, kind], part_rsem.at[side, kind],
-                device_id=near(1 - side), device_id_type=MESH,
-            ).wait()
+    for source in (1, 2):
+        for q in range(4):
+            hand_back(source, q).wait()
+        pltpu.make_async_remote_copy(
+            score_send.at[source - 1], score_recv.at[source - 1],
+            part_ssem.at[source - 1, 4], part_rsem.at[source - 1, 4],
+            device_id=near(2 - source), device_id_type=MESH,
+        ).wait()
     gtok_ref[...] = (
         total[0] + part_recv[0].astype(F32) + part_recv[1].astype(F32)
     ).astype(BF16)
@@ -504,7 +517,7 @@
             pltpu.SemaphoreType.REGULAR((6,)),
             dma((13,)), dma((2, 3)), dma((2, 3)), dma((4, 3)),
             dma((2, CHUNKS)), dma((2, CHUNKS)), dma((CHUNKS,)), dma((CHUNKS,)),
-            dma((CHUNKS,)), dma((CHUNKS,)), dma((2, 2)), dma((2, 2)), dma, dma,
+            dma((CHUNKS,)), dma((CHUNKS,)), dma((2, 5)), dma((2, 5)), dma, dma,
         ],
         compiler_params=pltpu.CompilerParams(
             collective_id=0, has_side_effects=True, vmem_limit_bytes=60 * 2**20

time: 73.2 us -> 73 us (level)
  no operation moved by 1% of the time
where the time goes in v5:
time: 73 us; the launch traced here: 72.6 us
  Pallas kernels  71.8 us (98%)
  between operations  0.8 us (1%)
    pallas_call x1, Pallas kernels, body(): pl.pallas_call(kernel, out_shape=(pltpu.VMEM((TOK, D), BF16), pltpu.VMEM(...  70.4 us

profile of v5, /device:TPU:2, one launch (start us, length us, event | category | flops | bytes accessed | tf_op | source)
XLA Modules:
  0.0 72.6 jit_solution(7485446982911095829)
XLA Ops:
  0.6 70.4 %shard_map.102 = (bf16[128,1024]{1,0:T(8,128)(2,1)S(1)}, f32[2,128]{1,0:T(2,128)S(1)}, bf16[1,1024,512]{2,1,0:T(8,128)(2,1)S(1)}, bf16[1,1024,512]{2,1,0:T(8,128)(2,1)S(1)}) custom-call(bf16[128,1024]{1,0:T(8,128)(2,1)} %tokens_hbm.1, bf16[128,1024]{1,0:T(8,128)(2,1)} %cot_hbm.1, f32[2,128]{1,0:T(2,128)} %bitcast.4, s32[2,128]{1,0:T(2,128)} %bitcast.5, ...), custom_call_target="tpu_custom_call" | custom-call | flops 6442450944 | bytes 7340032 | tf_op jit(solution)/shard_map/pallas_call | solution.py:475
  71.0 1.4 %shard_map.103 = (bf16[128,1024]{1,0:T(8,128)(2,1)}, f32[2,128]{1,0:T(2,128)}, bf16[1,1024,512]{2,1,0:T(8,128)(2,1)}, bf16[1,1024,512]{2,1,0:T(8,128)(2,1)}) custom-call(bf16[128,1024]{1,0:T(8,128)(2,1)S(1)} %get-tuple-element.12.refs_0_, f32[2,128]{1,0:T(2,128)S(1)} %get-tuple-element.13.refs_1_, bf16[1,1024,512]{2,1,0:T(8,128)(2,1)S(1)} %get-tuple-element.14.refs_2_, ...), custom_call_target="tpu_custom_call" | custom-call | tf_op jit(solution)/shard_map/pallas_call | solution.py:537
